TPU v7x, 512 devices: a whole 4x4x16 slice. The times are simulated.
512 devices in a mesh: img: 128 (over y, z, core), tp: 4 (over x).
Axes of the slice: x: 4, y: 4, z: 16, core: 2. Of those that a mesh axis runs over, the one named last changes fastest.
Arguments:
- encoded: bfloat16 [2048, 8, 1024], P('img'), may hold values from -6 to 6
- pair_images: int32 [4096, 2], replicated, may hold values from 0 to 2047, as said below
- embed_w: bfloat16 [1024, 768], replicated, may hold values from -0.1875 to 0.1875
- gain_query: bfloat16 [768], replicated, may hold values from 0.099609375 to 1.8984375
- gain_key: bfloat16 [768], replicated, may hold values from 0.099609375 to 1.8984375
- gain_out: bfloat16 [768], replicated, may hold values from 0.099609375 to 1.8984375
- w_query: bfloat16 [768, 768], P(None, 'tp'), may hold values from -3 to 3
- w_key: bfloat16 [768, 768], P(None, 'tp'), may hold values from -3 to 3
- w_value: bfloat16 [768, 768], P(None, 'tp'), may hold values from -0.21875 to 0.21875
- w_out: bfloat16 [768, 768], P('tp'), may hold values from -0.21875 to 0.21875
- head_w: bfloat16 [768, 1024], P('tp'), may hold values from -0.21875 to 0.21875
Outputs:
- pointmaps: bfloat16 [2048, 8, 1024], P('img', None, 'tp')
Inputs may be any that keep to these rules, and one draw needn't show every extreme that they name: `pair_images`: A global image id is owner index times 16 plus the position among that owner's images. Worker w runs pairs w * 32 to (w + 1) * 32 - 1. The 64 images named in one worker's pairs are all different, and at most 1 of them lie on one owner; in every draw some owner holds exactly 1 of them. The two images of a pair lie on different owners.
All inputs are finite; a program needn't handle non-finite values.
Results may differ from a plain program's by a relative error of at most 0.02.
Values may be sent and summed in bfloat16 or wider, within the bound.
A program may use at most 64 MiB of HBM per device.

v0:
```python
import jax
import jax.numpy as jnp
from jax import lax
from jax.sharding import PartitionSpec as P

HEAD_DIM = 64


def layer_norm(values, gain):
    center = values - jnp.mean(values, axis=-1, keepdims=True)
    spread = jnp.mean(center * center, axis=-1, keepdims=True)
    return center * lax.rsqrt(spread + 1e-06) * gain.astype(jnp.float32)


def select_rows(selector, source):
    flat = source.reshape(source.shape[0], -1)
    picked = jnp.dot(
        selector.astype(jnp.bfloat16), flat, preferred_element_type=jnp.float32
    ).astype(jnp.bfloat16)
    return picked.reshape((selector.shape[0],) + source.shape[1:])


def shards(
    encoded,
    pair_images,
    embed_w,
    gain_query,
    gain_key,
    gain_out,
    w_query,
    w_key,
    w_value,
    w_out,
    head_w,
):
    owner_count = lax.axis_size("img")
    owner_self = lax.axis_index("img")
    group_count = lax.axis_size("tp")
    group_self = lax.axis_index("tp")
    images_here = encoded.shape[0]
    tokens_img = encoded.shape[1]
    width = embed_w.shape[1]
    group_w = width // group_count
    view_count = pair_images.shape[0] // owner_count * 2
    slot_cap = max(1, view_count // owner_count)
    table = pair_images.reshape(owner_count, view_count)
    view_index = jnp.arange(view_count, dtype=jnp.int32)
    before = view_index[:, None] < view_index[None, :]
    owner_table = table // images_here
    hits = owner_table == owner_self
    rank_all = jnp.sum((hits[:, :, None] & before[None, :, :]).astype(jnp.int32), axis=1)
    slot_hot = (
        hits[:, :, None]
        & (rank_all[:, :, None] == jnp.arange(slot_cap, dtype=jnp.int32)[None, None, :])
    ).astype(jnp.float32)
    positions = jnp.arange(images_here, dtype=jnp.int32)
    image_hot = ((table % images_here)[:, :, None] == positions[None, None, :]).astype(jnp.float32)
    outgoing = jnp.einsum("wvk,wvi->wki", slot_hot, image_hot).reshape(
        owner_count * slot_cap, images_here
    )
    my_ids = lax.dynamic_index_in_dim(table, owner_self, 0, keepdims=False)
    my_owners = my_ids // images_here
    same_owner = my_owners[:, None] == my_owners[None, :]
    my_rank = jnp.sum((same_owner & before).astype(jnp.int32), axis=0)
    slot_of = my_owners * slot_cap + my_rank
    incoming = (
        slot_of[:, None] == jnp.arange(owner_count * slot_cap, dtype=jnp.int32)[None, :]
    ).astype(jnp.float32)
    enc_width = encoded.shape[2] // group_count
    local = lax.dynamic_slice_in_dim(encoded, group_self * enc_width, enc_width, 2)
    received = lax.all_to_all(
        select_rows(outgoing, local), "img", split_axis=0, concat_axis=0, tiled=True
    )
    view_part = select_rows(incoming, received)
    enc_views = lax.all_gather(view_part, "tp", axis=2, tiled=True)
    views = jnp.dot(enc_views, embed_w, preferred_element_type=jnp.float32).astype(jnp.bfloat16)
    base_norm = layer_norm(views.astype(jnp.float32), jnp.ones((width,), jnp.float32))
    swapped = base_norm.reshape(view_count // 2, 2, tokens_img, width)[:, ::-1].reshape(
        view_count, tokens_img, width
    )
    normed_q = (base_norm * gain_query.astype(jnp.float32)).astype(jnp.bfloat16)
    normed_k = (swapped * gain_key.astype(jnp.float32)).astype(jnp.bfloat16)
    query = (
        jnp.dot(normed_q, w_query, preferred_element_type=jnp.float32) * HEAD_DIM ** (-0.5)
    ).astype(jnp.bfloat16)
    keys = jnp.dot(normed_k, w_key, preferred_element_type=jnp.float32).astype(jnp.bfloat16)
    values = jnp.dot(normed_k, w_value, preferred_element_type=jnp.float32).astype(jnp.bfloat16)
    heads_here = group_w // HEAD_DIM
    query = query.reshape(view_count, tokens_img, heads_here, HEAD_DIM)
    keys = keys.reshape(view_count, tokens_img, heads_here, HEAD_DIM)
    values = values.reshape(view_count, tokens_img, heads_here, HEAD_DIM)
    scores = jnp.einsum("vqhd,vkhd->vhqk", query, keys, preferred_element_type=jnp.float32)
    weights = jax.nn.softmax(scores, axis=-1).astype(jnp.bfloat16)
    attended = jnp.einsum(
        "vhqk,vkhd->vqhd", weights, values, preferred_element_type=jnp.float32
    ).astype(jnp.bfloat16)
    attended = attended.reshape(view_count, tokens_img, group_w)
    partial_mix = jnp.dot(attended, w_out, preferred_element_type=jnp.float32)
    mixed = lax.psum(partial_mix.astype(jnp.bfloat16), "tp").astype(jnp.float32)
    hidden = views.astype(jnp.float32) + mixed
    normed = layer_norm(hidden, gain_out).astype(jnp.bfloat16)
    share = lax.dynamic_slice_in_dim(normed, group_self * group_w, group_w, 2)
    returned = lax.all_to_all(
        select_rows(incoming.T, share), "img", split_axis=0, concat_axis=0, tiled=True
    )
    flat_back = returned.reshape(owner_count * slot_cap, -1)
    summed = jnp.dot(outgoing.T.astype(jnp.bfloat16), flat_back, preferred_element_type=jnp.float32)
    summed = summed.astype(jnp.bfloat16).reshape(images_here, tokens_img, group_w)
    head_terms = jnp.dot(summed, head_w, preferred_element_type=jnp.float32)
    return lax.psum_scatter(head_terms.astype(jnp.bfloat16), "tp", scatter_dimension=2, tiled=True)


def solution(mesh):
    placed = (
        P("img", None, None),
        P(),
        P(),
        P(),
        P(),
        P(),
        P(None, "tp"),
        P(None, "tp"),
        P(None, "tp"),
        P("tp", None),
        P("tp", None),
    )
    return jax.shard_map(
        shards, mesh=mesh, in_specs=placed, out_specs=P("img", None, "tp"), check_vma=False
    )
```

profile of v0, /device:TPU:1, one launch (start us, length us, event | category | flops | bytes accessed | tf_op | source)
XLA Modules:
  0.0 262.4 jit_solution(15759082420801121636)
XLA Ops:
  6.6 1.0 constant_dynamic-slice_fusion
  7.5 2.8 %copy.40 = s32[4096,2]{1,0:T(8,128)} copy(s32[4096,2]{0,1:T(2,128)} %param.12) | data formatting | bytes 65536 | tf_op args[1]
  10.3 3.2 %reshape.185 = s32[128,64]{1,0:T(8,128)S(1)} reshape(s32[4096,2]{1,0:T(8,128)} %copy.40) | data formatting | bytes 65536 | tf_op jit(solution)/shard_map/reshape | solution.py:46
  13.6 0.7 convert_reduce_fusion.1
  14.6 0.3 convolution_convert_fusion.1
  14.9 0.9 copy.65
  15.8 20.6 %all-to-all-start = ((bf16[128,8,256]{2,1,0:T(8,128)(2,1)}), bf16[128,8,256]{2,1,0:T(8,128)(2,1)S(1)}, u32[]{:S(2)}, u32[]{:S(2)}) async-start(bf16[128,8,256]{2,1,0:T(8,128)(2,1)} %bitcast.20), calls=%async_computation | async-start | bytes 1048576 | tf_op jit(solution)/shard_map/all_to_all | solution.py:71
  36.6 33.0 %all-to-all-done = bf16[128,8,256]{2,1,0:T(8,128)(2,1)S(1)} async-done(((bf16[128,8,256]{2,1,0:T(8,128)(2,1)}), bf16[128,8,256]{2,1,0:T(8,128)(2,1)S(1)}, u32[]{:S(2)}, u32[]{:S(2)}) %all-to-all-start) | async-done | bytes 524320 | tf_op jit(solution)/shard_map/all_to_all | solution.py:71
  69.7 0.3 convolution_convert_fusion.2
  70.0 0.8 copy.67
  70.8 0.2 all-reduce.2.cloned.1.call-start
  71.0 24.4 %all-gather.2.cloned.1.call-done = bf16[64,8,1024]{2,1,0:T(8,128)(2,1)} async-done(((bf16[64,8,256]{2,1,0:T(8,128)(2,1)}), bf16[64,8,1024]{2,1,0:T(8,128)(2,1)}) %all-gather.2.cloned.1.call-update) | async-done | bytes 1048592 | tf_op jit(solution)/shard_map/all_gather | solution.py:75
  95.5 2.3 convert_reduce_fusion
  97.8 0.4 fusion.3
  98.2 0.6 copy-done.11
  98.8 1.4 fusion.1
  100.2 2.7 %rev.3 = f32[32,2,8,768]{3,2,1,0:T(8,128)} reverse(f32[32,2,8,768]{3,2,1,0:T(8,128)} %bitcast.71), dimensions={1} | reverse | bytes 3145728 | tf_op jit(solution)/shard_map/rev | solution.py:78
  102.9 1.6 fusion.4
  104.5 1.1 convolution_convert_fusion.8
  105.6 1.2 copy.45
  106.8 1.0 copy.50
  107.8 2.1 fusion.14
  109.9 1.2 copy.46
  111.1 1.0 copy.48
  112.1 2.1 convolution_convert_fusion.7
  114.2 1.2 copy.47
  115.4 0.2 copy.49
  115.7 0.3 fusion.36
  116.1 0.9 copy-done.3
  116.9 0.5 fusion.35
  117.4 1.9 fusion.15
  119.4 0.3 copy.52
  119.7 0.3 copy.53
  120.0 0.4 copy-done.8
  120.3 1.3 convolution_convert_fusion.4
  121.8 59.9 %all-reduce.2.cloned.1.call-done = bf16[64,8,768]{2,1,0:T(8,128)(2,1)} async-done(((bf16[64,8,768]{2,1,0:T(8,128)(2,1)}), bf16[64,8,768]{2,1,0:T(8,128)(2,1)}) %all-reduce.2.cloned.1.call-update) | async-done | bytes 786448 | tf_op jit(solution)/shard_map/psum | solution.py:99
  181.7 1.5 fusion.8
  183.2 0.4 multiply_reduce_fusion
  183.6 0.3 fusion.18
  183.9 0.2 reshape.196
  184.2 0.2 convolution_convert_fusion
  184.4 0.2 copy.54
  184.6 0.4 copy.55
  185.0 51.4 %all_to_all.10 = bf16[128,8,192]{2,1,0:T(8,128)(2,1)S(1)} all-to-all(bf16[128,8,192]{2,1,0:T(8,128)(2,1)S(1)} %copy.55), channel_id=1, replica_groups=mesh['img'=128,'tp'=4] {'img'}, dimensions={0} | all-to-all | bytes 786432 | tf_op jit(solution)/shard_map/all_to_all | solution.py:103
  236.5 0.4 copy.56
  236.9 0.2 convolution_convert_fusion.3
  237.3 0.9 convolution_convert_fusion.6
  238.2 17.6 %reduce-scatter.2.cloned.1.call-done = bf16[16,8,256]{2,1,0:T(8,128)(2,1)} async-done(((bf16[16,8,1024]{2,1,0:T(8,128)(2,1)}), bf16[16,8,256]{2,1,0:T(8,128)(2,1)}) %reduce-scatter.2.cloned.1.call-update) | async-done | bytes 65552 | tf_op jit(solution)/shard_map/reduce_scatter | solution.py:110
  (53 shorter events, 1.1 us)
Async XLA Ops:
  6.5 88.9 %copy-start = (bf16[1024,768]{1,0:T(8,128)(2,1)S(1)}, bf16[1024,768]{1,0:T(8,128)(2,1)}, u32[]{:S(2)}) copy-start(bf16[1024,768]{1,0:T(8,128)(2,1)} %param.13) | copy-start | bytes 4718596
  14.6 1.2 copy-start.9
  15.8 53.8 %all-to-all-start = ((bf16[128,8,256]{2,1,0:T(8,128)(2,1)}), bf16[128,8,256]{2,1,0:T(8,128)(2,1)S(1)}, u32[]{:S(2)}, u32[]{:S(2)}) async-start(bf16[128,8,256]{2,1,0:T(8,128)(2,1)} %bitcast.20), calls=%async_computation | async-start | bytes 1048576 | tf_op jit(solution)/shard_map/all_to_all | solution.py:71
  36.4 34.6 %copy-start.12 = (bf16[768]{0:T(1024)(128)(2,1)S(1)}, bf16[768]{0:T(1024)(128)(2,1)}, u32[]{:S(2)}) copy-start(bf16[768]{0:T(1024)(128)(2,1)} %param.15) | copy-start | bytes 4612
  36.4 34.6 %copy-start.13 = (bf16[768]{0:T(1024)(128)(2,1)S(1)}, bf16[768]{0:T(1024)(128)(2,1)}, u32[]{:S(2)}) copy-start(bf16[768]{0:T(1024)(128)(2,1)} %param.14) | copy-start | bytes 4612
  36.4 59.1 %all-gather.2.cloned.1.call-start = ((), (), s32[]{:S(2)}) async-start(), calls=%async_computation.3 | async-start | bytes 1310720 | tf_op jit(solution)/shard_map/all_gather | solution.py:75
  70.8 110.9 %all-reduce.2.cloned.1.call-start = ((), (), s32[]{:S(2)}) async-start(), calls=%async_computation.4 | async-start | bytes 1572864 | tf_op jit(solution)/shard_map/psum | solution.py:99
  97.8 2.5 copy-start.6
  98.2 0.6 copy-start.11
  102.9 1.6 copy-start.7
  112.1 3.6 %copy-start.2 = (bf16[64,8,3,64]{3,1,2,0:T(8,128)(2,1)S(1)}, bf16[64,8,3,64]{3,1,2,0:T(8,128)(2,1)}, u32[]{:S(2)}) copy-start(bf16[64,8,3,64]{3,1,2,0:T(8,128)(2,1)} %copy.48) | copy-start | bytes 589828
  115.7 1.7 copy-start.4
  116.0 0.9 copy-start.3
  119.4 1.0 copy-start.8
  119.7 2.0 copy-start.14
  121.6 134.3 %reduce-scatter.2.cloned.1.call-start = ((), (), s32[]{:S(2)}) async-start(), calls=%async_computation.5 | async-start | bytes 327680 | tf_op jit(solution)/shard_map/reduce_scatter | solution.py:110
  181.7 1.5 copy-start.1
  184.6 52.3 %copy-start.10 = (bf16[128,16]{1,0:T(8,128)(2,1)S(1)}, bf16[128,16]{1,0:T(8,128)(2,1)}, u32[]{:S(2)}) copy-start(bf16[128,16]{1,0:T(8,128)(2,1)} %copy-done.9) | copy-start | bytes 12292
  184.6 52.7 %copy-start.5 = (bf16[192,1024]{1,0:T(8,128)(2,1)S(1)}, bf16[192,1024]{1,0:T(8,128)(2,1)}, u32[]{:S(2)}) copy-start(bf16[192,1024]{1,0:T(8,128)(2,1)} %param.21) | copy-start | bytes 1179652
Sparse Core Ops, SparseCore 0:
  70.9 24.5 all-gather.1
  121.8 59.8 all-reduce.1
  238.4 17.4 reduce-scatter.1
where the time goes:
time: 264 us; the launch traced here: 262 us
  waiting for transfers between devices  135 us (51%)
  blocking collectives  51.4 us (19%)
  local copies, waits for them, and re-layouts  21.4 us (8%)
  starting transfers between devices  20.9 us (8%)
  between operations  13.5 us (5%)
  matrix products  13 us (5%)
  other arithmetic  7.15 us (3%)
    psum x1, waiting for transfers between devices, shards(): mixed = lax.psum(partial_mix.astype(jnp.bfloat16), 'tp').astype(jnp.float32)  59.9 us
    all_to_all x1, blocking collectives, shards(): lax.all_to_all(select_rows(incoming.T, share), 'img', split_axis=0, conca...  51.4 us
    all_to_all x1, waiting for transfers between devices, shards(): lax.all_to_all(select_rows(outgoing, local), 'img', split_axis=0, concat_...  33 us
    all_gather x1, waiting for transfers between devices, shards(): enc_views = lax.all_gather(view_part, 'tp', axis=2, tiled=True)  24.4 us
    all_to_all x1, starting transfers between devices, shards(): lax.all_to_all(select_rows(outgoing, local), 'img', split_axis=0, concat_...  20.6 us
    reduce_scatter x1, waiting for transfers between devices, shards(): lax.psum_scatter(head_terms.astype(jnp.bfloat16), 'tp', scatter_dimension...  17.6 us
    unnamed x35, local copies, waits for them, and re-layouts  6.45 us
  transfers between devices with their start and end apart: 4, of which 4 were waited for; matrix products, arithmetic and copies ran while one was open for 0% of the time, Pallas kernels for 0%

commit v1 on v0

v1 whole, which is shorter than its diff:
```python
import functools

import jax
import jax.numpy as jnp
from jax import lax
from jax.experimental import pallas as pl
from jax.experimental.pallas import tpu as pltpu
from jax.sharding import PartitionSpec as P

HEAD_DIM = 64
GRID = (4, 16, 2)
LANES = 128
MESH = pl.DeviceIdType.MESH
F32 = jnp.float32
BF16 = jnp.bfloat16


def iota(shape, dim):
    return lax.broadcasted_iota(jnp.int32, shape, dim)


def dot(a, b):
    return jnp.dot(a, b, preferred_element_type=F32)


def dot_t(a, b):
    return lax.dot_general(a, b, (((1,), (1,)), ((), ())), preferred_element_type=F32)


def one_hot(condition):
    return jnp.where(condition, 1.0, 0.0)


def norm_base(values):
    center = values - jnp.mean(values, axis=-1, keepdims=True)
    spread = jnp.mean(center * center, axis=-1, keepdims=True)
    return center * lax.rsqrt(spread + 1e-06)


def body(
    dims,
    enc_hbm,
    pairs_hbm,
    embed_hbm,
    gains_ref,
    wk_hbm,
    wv_hbm,
    wq_hbm,
    wo_hbm,
    head_hbm,
    out_ref,
    enc,
    pairs,
    embed,
    wqkv,
    wo,
    head,
    ag,
    yout,
    yr,
    xout,
    xr,
    nout,
    nr,
    uout,
    ur,
    zout,
    zr,
    oout,
    qsum,
    in_sem,
    ag_send,
    ag_recv,
    y_send,
    y_recv,
    x_send,
    x_recv,
    n_send,
    n_recv,
    u_send,
    u_recv,
    z_send,
    z_recv,
    o_send,
    o_recv,
    w_send,
    w_recv,
):
    ny, nz, nc, tp, imgs, toks, tk, pairs_dev, pp, dm, gw, cols = dims
    nd = ny * nc
    de = enc.shape[1]
    views = 2 * pairs_dev
    rows = tp * tk * 2 * pp
    img = lax.axis_index("img")
    t = lax.axis_index("tp")
    c = lax.rem(img, nc)
    z = lax.rem(img // nc, nz)
    y = img // (nc * nz)
    d = y * nc + c

    def img_of(dd, zz):
        return (dd // nc) * (nz * nc) + zz * nc + lax.rem(dd, nc)

    def remote(src, dst, send, recv, device):
        return pltpu.make_async_remote_copy(
            src_ref=src, dst_ref=dst, send_sem=send, recv_sem=recv, device_id=device, device_id_type=MESH
        )

    loads = [
        pltpu.make_async_copy(src, dst, in_sem.at[i])
        for i, (src, dst) in enumerate(
            [
                (enc_hbm, enc),
                (embed_hbm, embed),
                (wk_hbm, wqkv.at[0, 0:gw]),
                (wv_hbm, wqkv.at[0, gw : 2 * gw]),
                (wq_hbm, wqkv.at[0, 2 * gw : 3 * gw]),
                (pairs_hbm, pairs),
                (wo_hbm, wo.at[0]),
                (head_hbm, head.at[t]),
            ]
        )
    ]
    for load in loads:
        load.start()

    barrier = pltpu.get_barrier_semaphore()
    partners = (
        [(img_of(d, lax.rem(z + k, nz)), t) for k in range(1, nz)]
        + [(img_of(lax.rem(d + r, nd), z), t) for r in range(1, nd)]
        + [(img, lax.rem(t + r, tp)) for r in range(1, tp)]
    )
    for partner in partners:
        pl.semaphore_signal(barrier, inc=1, device_id=partner, device_id_type=MESH)

    row, col = iota((tk * imgs, imgs * toks), 0), iota((tk * imgs, imgs * toks), 1)
    pick = one_hot(col == lax.rem(row, imgs) * toks + t * tk + row // imgs).astype(BF16)
    loads[0].wait()
    mine = dot(pick, enc[...]).astype(BF16)
    loads[1].wait()
    ag[0] = dot(mine, embed[...]).astype(BF16).reshape(tk, imgs, dm)

    pl.semaphore_wait(barrier, len(partners))

    half = nz // 2
    up_dev = (img_of(d, lax.rem(z + 1, nz)), t)
    down_dev = (img_of(d, lax.rem(z + nz - 1, nz)), t)
    ring = {}
    for s in range(1, half + 1):
        for ch in range(tk):
            if s < half or ch % 2 == 0:
                ring[0, s, ch] = remote(
                    ag.at[(nz - s + 1) % nz, ch],
                    ag.at[nz - s, ch],
                    ag_send.at[0, s - 1, ch],
                    ag_recv.at[0, s - 1, ch],
                    up_dev,
                )
            if s < half or ch % 2 == 1:
                ring[1, s, ch] = remote(
                    ag.at[s - 1, ch], ag.at[s, ch], ag_send.at[1, s - 1, ch], ag_recv.at[1, s - 1, ch], down_dev
                )

    def ring_start(s):
        for ch in range(tk):
            for way in range(2):
                if (way, s, ch) in ring:
                    if s > 1:
                        ring[way, s - 1, ch].wait_recv()
                    ring[way, s, ch].start()

    ring_start(1)

    next_t, prev_t = lax.rem(t + 1, tp), lax.rem(t + tp - 1, tp)
    far_t = lax.rem(t + 2, tp)
    sibling = (img_of(y * nc + (1 - c), z), t)

    def weight_copies(which, buf, own, before, after, far, own_after, own_before, far_slot):
        quarter = buf.shape[1] // 4

        def part(slot, u):
            return buf.at[slot, pl.ds(pl.multiple_of((2 * c + u) * quarter, quarter), quarter)]

        out = {}

        def add(name, src, dst, device):
            i = len(out)
            out[name] = remote(src, dst, w_send.at[which, i], w_recv.at[which, i], device)

        for u in range(2):
            add(("up", u), part(own, u), part(own_after, u), (img, next_t))
            add(("down", u), part(own, u), part(own_before, u), (img, prev_t))
        add("fwd_up", part(before, 0), part(far_slot, 0), (img, next_t))
        add("fwd_down", part(after, 1), part(far_slot, 1), (img, prev_t))
        for u in range(2):
            add(("sib_before", u), part(before, u), part(before, u), sibling)
            add(("sib_after", u), part(after, u), part(after, u), sibling)
            add(("sib_far", u), part(far, u), part(far, u), sibling)
        return out

    w_qkv = weight_copies(0, wqkv, 0, 3, 1, 2, 3, 1, 2)
    w_out = weight_copies(1, wo, 0, 3, 1, 2, 3, 1, 2)

    def head_part(slot, u):
        quarter = head.shape[1] // 4
        return head.at[slot, pl.ds(pl.multiple_of((2 * c + u) * quarter, quarter), quarter)]

    w_head = {}

    def add_head(name, slot, u, device):
        i = len(w_head)
        w_head[name] = remote(head_part(slot, u), head_part(slot, u), w_send.at[2, i], w_recv.at[2, i], device)

    for u in range(2):
        add_head(("up", u), t, u, (img, next_t))
        add_head(("down", u), t, u, (img, prev_t))
    add_head("fwd_up", prev_t, 0, (img, next_t))
    add_head("fwd_down", next_t, 1, (img, prev_t))
    for u in range(2):
        add_head(("sib_before", u), prev_t, u, sibling)
        add_head(("sib_after", u), next_t, u, sibling)
        add_head(("sib_far", u), far_t, u, sibling)

    def first_sends(w):
        for u in range(2):
            w["up", u].start()
            w["down", 1 - u].start()

    def pass_on(w, u):
        w["up", u].wait_recv()
        if u == 0:
            w["fwd_up"].start()
        w["sib_before", u].start()
        w["down", 1 - u].wait_recv()
        if u == 0:
            w["fwd_down"].start()
        w["sib_after", 1 - u].start()

    def pass_far(w):
        w["fwd_up"].wait_recv()
        w["sib_far", 0].start()
        w["fwd_down"].wait_recv()
        w["sib_far", 1].start()

    def arrive(w, name):
        for u in range(2):
            w[name, u].wait_recv()

    for load in loads[2:5]:
        load.wait()
    first_sends(w_qkv)
    ring_start(2)
    loads[6].wait()
    first_sends(w_out)

    loads[5].wait()
    lanes = pairs.shape[2]
    z_par = lanes // (nc * pairs_dev)
    blocks_y = nz // z_par
    log_img = imgs.bit_length() - 1
    log_c = nc.bit_length() - 1
    log_z = nz.bit_length() - 1

    def parts_of(ids):
        owner = ids >> log_img
        return ids & (imgs - 1), owner & (nc - 1), (owner >> log_c) & (nz - 1), owner >> (log_c + log_z)

    def rel_z(zz):
        return (zz - z + nz) & (nz - 1)

    lane1 = iota((1, lanes), 1)
    lane_par, lane_core, lane_pair = lane1 // (nc * pairs_dev), (lane1 // pairs_dev) % nc, lane1 % pairs_dev
    my_par = lax.rem(z, z_par)
    my_block = z // z_par

    at_z = lane_par == my_par
    hots, spreads = [], []
    code_rows = iota((nz * imgs, lanes), 0)
    dest_rows = iota((nd * nz, lanes), 0) // nz
    for yy in range(ny):
        both = pairs[yy * blocks_y + my_block]
        hot = jnp.zeros((nz * imgs, lanes), F32)
        for side in range(2):
            im, oc, oz, oy = parts_of(both[side : side + 1])
            code = jnp.where(at_z & (oc == c) & (oy == y), rel_z(oz) * imgs + im, -1)
            hot = hot + one_hot(code_rows == code)
        hots.append(hot.astype(BF16))
        spreads.append(one_hot(dest_rows == yy * nc + lane_core).astype(BF16))
    gather_mat = sum(dot_t(spreads[yy], hots[yy]) for yy in range(ny))
    keep = iota((nd * nz, nz * imgs), 0) % nz == iota((nd * nz, nz * imgs), 1) // imgs
    gather_mat = jnp.where(keep, gather_mat, 0.0).astype(BF16)

    ring_start(3) if half >= 3 else None

    both = pairs[y * blocks_y + my_block]
    at_me = (lane_par == my_par) & (lane_core == c)
    slot_rows = iota((nd * nz, lanes), 0)
    view = iota((views, lanes), 0)
    view_pair = view // (2 * pp) * pp + view % pp
    view_side = (view // pp) % 2
    view_mat = jnp.zeros((views, nd * nz), F32)
    back_mat = jnp.zeros((nd * nz, views), F32)
    for side in range(2):
        im, oc, oz, oy = parts_of(both[side : side + 1])
        code = jnp.where(at_me, (oy * nc + oc) * nz + rel_z(oz), -1)
        slot_hot = one_hot(slot_rows == code).astype(BF16)
        view_hot = one_hot(at_me & (lane_pair == view_pair) & (view_side == side)).astype(BF16)
        view_mat = view_mat + dot_t(view_hot, slot_hot)
        back_mat = back_mat + dot_t(slot_hot, view_hot)
    view_mat = view_mat.astype(BF16)
    back_mat = back_mat.astype(BF16)

    for s in range(4, half + 1):
        ring_start(s)

        share = -(-(ny * blocks_y) // (half - 3))
        for block in range((s - 4) * share, min((s - 3) * share, ny * blocks_y)):
            yy, zb = block // blocks_y, block % blocks_y
            both = pairs[block]
            img_rows = iota((tk * imgs, lanes), 0) % imgs
            hot = jnp.zeros((tk * imgs, lanes), F32)
            for side in range(2):
                im, oc, oz, oy = parts_of(both[side : side + 1])
                code = jnp.where((oc == c) & (oy == y) & (oz == z), im, -1)
                hot = hot + one_hot(img_rows == code)
            from_k = rel_z(zb * z_par + lane_par)
            from_d = yy * nc + lane_core
            slot = iota((nz * tk * nd, lanes), 0)
            spread = one_hot((slot // (tk * nd) == from_k) & (slot % nd == from_d))
            term = dot_t(hot.astype(BF16), spread.astype(BF16))
            if block == 0:
                qsum[...] = term
            else:
                qsum[...] += term

    pass_on(w_qkv, 0)

    for ch in range(tk):
        for way in range(2):
            if (way, half, ch) in ring:
                ring[way, half, ch].wait_recv()
            else:
                ring[way, half - 1, ch].wait_recv()

    y_copies = {}
    for ch in range(tk):
        got = dot(gather_mat, ag[:, ch].reshape(nz * imgs, dm))
        yout[:, ch] = got.astype(BF16).reshape(nd, nz, dm)
        for r in range(1, nd):
            other = lax.rem(d + r, nd)
            y_copies[r, ch] = remote(
                yout.at[other, ch], yr.at[d, ch], y_send.at[r, ch], y_recv.at[r, ch], (img_of(other, z), t)
            )
            y_copies[r, ch].start()
    yr[d] = yout[d]

    pass_on(w_qkv, 1)
    pass_on(w_out, 0)

    x_copies = {}
    for ch in range(tk):
        for r in range(1, nd):
            y_copies[r, ch].wait_recv()
        got = dot(view_mat, yr[:, ch].reshape(nd * nz, dm))
        xout[:, ch] = got.astype(BF16).reshape(tp, 2 * pp, dm)
        for r in range(1, tp):
            other = lax.rem(t + r, tp)
            x_copies[r, ch] = remote(
                xout.at[other, ch], xr.at[t, ch], x_send.at[r, ch], x_recv.at[r, ch], (img, other)
            )
            x_copies[r, ch].start()
    xr[t] = xout[t]

    pass_far(w_qkv)
    pass_on(w_out, 1)
    pass_far(w_out)
    loads[7].wait()
    first_sends(w_head)

    for ch in range(tk):
        for r in range(1, tp):
            x_copies[r, ch].wait_recv()

    x = xr[...].reshape(rows, dm).astype(F32)
    base = norm_base(x)
    nq = (base * gains_ref[0:1, :]).astype(BF16)
    nk = (base * gains_ref[1:2, :]).astype(BF16)
    r0, r1 = iota((rows, rows), 0), iota((rows, rows), 1)
    seen = (r0 % pp == r1 % pp) & ((r0 // pp) % 2 != (r1 // pp) % 2)
    lane_head = iota((rows, gw), 1) // HEAD_DIM
    mixed = jnp.zeros((rows, dm), F32)
    for k, name in ((0, None), (3, "sib_before"), (1, "sib_after"), (2, "sib_far")):
        if name:
            arrive(w_qkv, name)
        keys = dot_t(nk, wqkv[k, 0:gw]).astype(BF16)
        values = dot_t(nk, wqkv[k, gw : 2 * gw]).astype(BF16)
        query = (dot_t(nq, wqkv[k, 2 * gw : 3 * gw]) * HEAD_DIM ** (-0.5)).astype(BF16)
        attended = jnp.zeros((rows, gw), F32)
        for h in range(gw // HEAD_DIM):
            here = lane_head == h
            scores = dot_t(jnp.where(here, query, jnp.zeros_like(query)), keys)
            scores = jnp.where(seen, scores, -1e38)
            raised = jnp.exp(scores - jnp.max(scores, axis=-1, keepdims=True))
            weights = raised / jnp.sum(raised, axis=-1, keepdims=True)
            attended = jnp.where(here, dot(weights.astype(BF16), values), attended)
        if name:
            arrive(w_out, name)
        mixed = mixed + dot(attended.astype(BF16), wo[k]).astype(BF16).astype(F32)
    normed = norm_base(x + mixed) * gains_ref[2:3, :]
    nout[...] = normed.astype(BF16).reshape(tp, tk, 2 * pp, dm)

    n_copies = {}
    for ch in range(tk):
        for r in range(1, tp):
            other = lax.rem(t + r, tp)
            n_copies[r, ch] = remote(
                nout.at[other, ch], nr.at[t, ch], n_send.at[r, ch], n_recv.at[r, ch], (img, other)
            )
            n_copies[r, ch].start()
    nr[t] = nout[t]

    pass_on(w_head, 0)

    u_copies = {}
    for ch in range(tk):
        for r in range(1, tp):
            n_copies[r, ch].wait_recv()
        got = dot(back_mat, nr[:, ch].reshape(views, dm))
        uout[:, ch] = got.astype(BF16).reshape(nd, nz, dm)
        for r in range(1, nd):
            other = lax.rem(d + r, nd)
            u_copies[r, ch] = remote(
                uout.at[other, ch], ur.at[d, ch], u_send.at[r, ch], u_recv.at[r, ch], (img_of(other, z), t)
            )
            u_copies[r, ch].start()
    ur[d] = uout[d]

    pass_on(w_head, 1)

    slot, other = iota((nz * nd, nz * nd), 0), iota((nz * nd, nz * nd), 1)
    turn = one_hot((slot // nd == other % nz) & (slot % nd == other // nz)).astype(BF16)
    turned = []
    for ch in range(tk):
        for r in range(1, nd):
            u_copies[r, ch].wait_recv()
        turned.append(dot(turn, ur[:, ch].reshape(nd * nz, dm)).reshape(nz, nd, dm))
    zout[...] = jnp.concatenate(turned, axis=1).astype(BF16)
    z_copies = []
    for k in [k for near in range(1, half + 1) for k in sorted({near, nz - near})]:
        copy = remote(
            zout.at[k], zr.at[nz - k], z_send.at[k], z_recv.at[k], (img_of(d, lax.rem(z + k, nz)), t)
        )
        copy.start()
        z_copies.append(copy)
    zr[0] = zout[0]

    pass_far(w_head)
    same = iota((tk * imgs, nz * tk * nd), 0) // imgs == (iota((tk * imgs, nz * tk * nd), 1) // nd) % tk
    sum_mat = jnp.where(same, qsum[...], 0.0).astype(BF16)
    for name in ("sib_before", "sib_after", "sib_far"):
        arrive(w_head, name)
    for copy in z_copies:
        copy.wait_recv()
    summed = dot(sum_mat, zr[...].reshape(nz * tk * nd, dm)).astype(BF16)
    maps = dot(summed, head[...].reshape(dm, tp * cols)).astype(BF16)
    for r in range(tp):
        oout[r] = maps[:, r * cols : (r + 1) * cols].reshape(tk, imgs, cols)
    o_copies = []
    for r in range(1, tp):
        other = lax.rem(t + r, tp)
        copy = remote(oout.at[other], out_ref.at[t], o_send.at[r], o_recv.at[r], (img, other))
        copy.start()
        o_copies.append(copy)
    out_ref[t] = oout[t]
    for copy in o_copies:
        copy.wait_recv()

    for copies in (ring, y_copies, x_copies, n_copies, u_copies, w_qkv, w_out, w_head):
        for copy in copies.values():
            copy.wait_send()
    for copy in z_copies + o_copies:
        copy.wait_send()


def shards(
    encoded,
    pair_images,
    embed_w,
    gain_query,
    gain_key,
    gain_out,
    w_query,
    w_key,
    w_value,
    w_out,
    head_w,
):
    ny, nz, nc = GRID
    tp = lax.axis_size("tp")
    owners = lax.axis_size("img")
    imgs, toks, de = encoded.shape
    dm = embed_w.shape[1]
    gw = dm // tp
    tk = toks // tp
    pairs_dev = pair_images.shape[0] // owners
    pp = pairs_dev // tp
    cols = head_w.shape[1] // tp
    nd = ny * nc
    views = 2 * pairs_dev
    lanes = min(LANES, nz * nc * pairs_dev)
    blocks = pair_images.shape[0] // lanes
    pairs = pair_images.reshape(blocks, lanes, 2).transpose(0, 2, 1)
    gains = jnp.stack([gain_query, gain_key, gain_out]).astype(F32)
    dims = (ny, nz, nc, tp, imgs, toks, tk, pairs_dev, pp, dm, gw, cols)
    hbm = pl.BlockSpec(memory_space=pl.ANY)
    vmem = pl.BlockSpec(memory_space=pltpu.VMEM)
    dma = pltpu.SemaphoreType.DMA
    swap_y = (nd, tk, nz, dm)
    swap_x = (tp, tk, 2 * pp, dm)
    out = pl.pallas_call(
        functools.partial(body, dims),
        name="sublayer",
        out_shape=jax.ShapeDtypeStruct((tp, tk, imgs, cols), BF16),
        in_specs=[hbm, hbm, hbm, vmem, hbm, hbm, hbm, hbm, hbm],
        out_specs=vmem,
        scratch_shapes=[
            pltpu.VMEM((imgs * toks, de), BF16),
            pltpu.VMEM(pairs.shape, jnp.int32),
            pltpu.VMEM(embed_w.shape, BF16),
            pltpu.VMEM((tp, 3 * gw, dm), BF16),
            pltpu.VMEM((tp, gw, dm), BF16),
            pltpu.VMEM((tp, gw, tp * cols), BF16),
            pltpu.VMEM((nz, tk, imgs, dm), BF16),
            pltpu.VMEM(swap_y, BF16),
            pltpu.VMEM(swap_y, BF16),
            pltpu.VMEM(swap_x, BF16),
            pltpu.VMEM(swap_x, BF16),
            pltpu.VMEM(swap_x, BF16),
            pltpu.VMEM(swap_x, BF16),
            pltpu.VMEM(swap_y, BF16),
            pltpu.VMEM(swap_y, BF16),
            pltpu.VMEM((nz, tk * nd, dm), BF16),
            pltpu.VMEM((nz, tk * nd, dm), BF16),
            pltpu.VMEM((tp, tk, imgs, cols), BF16),
            pltpu.VMEM((tk * imgs, nz * tk * nd), F32),
            dma((8,)),
            dma((2, nz // 2, tk)),
            dma((2, nz // 2, tk)),
            dma((nd, tk)),
            dma((nd, tk)),
            dma((tp, tk)),
            dma((tp, tk)),
            dma((tp, tk)),
            dma((tp, tk)),
            dma((nd, tk)),
            dma((nd, tk)),
            dma((nz,)),
            dma((nz,)),
            dma((tp,)),
            dma((tp,)),
            dma((3, 12)),
            dma((3, 12)),
        ],
        compiler_params=pltpu.CompilerParams(
            collective_id=0, has_side_effects=True, vmem_limit_bytes=48 * 1024 * 1024
        ),
    )(
        encoded.reshape(imgs * toks, de),
        pairs,
        embed_w,
        gains,
        w_key.T,
        w_value.T,
        w_query.T,
        w_out,
        head_w,
    )
    return out.reshape(toks, imgs, cols).transpose(1, 0, 2)


def solution(mesh):
    placed = (
        P("img", None, None),
        P(),
        P(),
        P(),
        P(),
        P(),
        P(None, "tp"),
        P(None, "tp"),
        P(None, "tp"),
        P("tp", None),
        P("tp", None),
    )
    return jax.shard_map(
        shards, mesh=mesh, in_specs=placed, out_specs=P("img", None, "tp"), check_vma=False
    )
```

time: 264 us -> 108 us (0.41)
  waiting for transfers between devices: 135 us -> 0 us
  Pallas kernels: 0 us -> 95.7 us
  blocking collectives: 51.4 us -> 0 us
  starting transfers between devices: 20.9 us -> 0 us
  between operations: 13.5 us -> 0.03 us
  matrix products: 13 us -> 0 us
  local copies, waits for them, and re-layouts: 21.4 us -> 10.7 us
  other arithmetic: 7.15 us -> 0.02 us
    pallas_call x0 -> x1, Pallas kernels: none -> 95.7 us  [shards(): pl.pallas_call(functools.partial(body, dims), name='sublayer', out_shape=...]
    psum x1 -> x0, waiting for transfers between devices: 59.9 us -> none  [shards(): mixed = lax.psum(partial_mix.astype(jnp.bfloat16), 'tp').astype(jnp.float32)]
    all_to_all x1 -> x0, blocking collectives: 51.4 us -> none  [shards(): lax.all_to_all(select_rows(incoming.T, share), 'img', split_axis=0, conca...]
    all_to_all x1 -> x0, waiting for transfers between devices: 33 us -> none  [shards(): lax.all_to_all(select_rows(outgoing, local), 'img', split_axis=0, concat_...]
    all_gather x1 -> x0, waiting for transfers between devices: 24.4 us -> none  [shards(): enc_views = lax.all_gather(view_part, 'tp', axis=2, tiled=True)]
    all_to_all x1 -> x0, starting transfers between devices: 20.6 us -> none  [shards(): lax.all_to_all(select_rows(outgoing, local), 'img', split_axis=0, concat_...]
    reduce_scatter x1 -> x0, waiting for transfers between devices: 17.6 us -> none  [shards(): lax.psum_scatter(head_terms.astype(jnp.bfloat16), 'tp', scatter_dimension...]
    dot_general x12 -> x0, matrix products: 13 us -> none  [the longest x1 2.29 us: shards(): jnp.dot(enc_views, embed_w, preferred_element_type=jnp.float32)]
  transfers between devices with their start and end apart: 4 -> 0, of which waited for: 4 -> 0; matrix products, arithmetic and copies ran while one was open for 0% -> 0% of each run, Pallas kernels for 0% -> 0%
where the time goes in v1:
time: 108 us; the launch traced here: 106 us
  Pallas kernels  95.7 us (89%)
  local copies, waits for them, and re-layouts  10.7 us (10%)
    pallas_call x1, Pallas kernels, shards(): pl.pallas_call(functools.partial(body, dims), name='sublayer', out_shape=...  95.7 us
    unnamed x16, local copies, waits for them, and re-layouts  7.95 us

profile of v1, /device:TPU:1, one launch (start us, length us, event | category | flops | bytes accessed | tf_op | source)
XLA Modules:
  0.0 106.4 jit_solution(13337469271992578249)
XLA Ops:
  0.0 0.7 stack.12
  0.7 0.7 stack.13
  1.4 0.7 stack.14
  2.1 0.0 copy-start
  2.1 1.4 %copy-done = bf16[1024,768]{1,0:T(8,128)(2,1)S(1)} copy-done((bf16[1024,768]{1,0:T(8,128)(2,1)S(1)}, bf16[1024,768]{1,0:T(8,128)(2,1)}, u32[]{:S(2)}) %copy-start) | copy-done | bytes 1572888
  3.5 0.0 copy-start.1
  3.5 1.0 copy-done.1
  4.5 0.0 copy-start.2
  4.5 1.0 copy-done.2
  5.4 0.0 copy-start.3
  5.4 1.0 copy-done.3
  6.4 0.0 copy-start.4
  6.4 1.0 copy-done.4
  7.4 0.0 copy-start.5
  7.4 1.0 copy-done.5
  8.3 0.0 copy-start.6
  8.3 0.9 copy-done.6
  9.3 0.0 copy-start.7
  9.3 0.8 copy-done.7
  10.0 95.7 %sublayer.1 = bf16[4,2,16,256]{3,2,1,0:T(8,128)(2,1)S(1)} custom-call(bf16[128,1024]{1,0:T(8,128)(2,1)S(1)} %bitcast.15, s32[32,2,128]{2,1,0:T(2,128)S(1)} %bitcast.16, bf16[1024,768]{1,0:T(8,128)(2,1)S(1)} %copy-done, f32[3,768]{1,0:T(4,128)S(1)} %maximum_convert_fusion.gains_ref, bf16[192,768]{1,0:T(8,128)(2,1)S(1)} %bitcast.11, ...), custom_call_target="tpu_custom_call" | custom-call | tf_op jit(solution)/shard_map/sublayer/pallas_call | solution.py:520
  105.8 0.7 copy.14
  (1 shorter events, 0.0 us)
Async XLA Ops:
  2.1 1.4 %copy-start = (bf16[1024,768]{1,0:T(8,128)(2,1)S(1)}, bf16[1024,768]{1,0:T(8,128)(2,1)}, u32[]{:S(2)}) copy-start(bf16[1024,768]{1,0:T(8,128)(2,1)} %embed_hbm.1) | copy-start | bytes 4718596
  3.5 1.0 copy-start.1
  4.5 1.0 copy-start.2
  5.4 1.0 copy-start.3
  6.4 1.0 copy-start.4
  7.4 1.0 copy-start.5
  8.3 0.9 copy-start.6
  9.3 0.8 copy-start.7

commit v2 on v1

v2 whole, which is shorter than its diff:
```python
import functools

import jax
import jax.numpy as jnp
from jax import lax
from jax.experimental import pallas as pl
from jax.experimental.pallas import tpu as pltpu
from jax.sharding import PartitionSpec as P

HEAD_DIM = 64
GRID = (4, 16, 2)
LANES = 128
CHUNKS = 2
MESH = pl.DeviceIdType.MESH
F32 = jnp.float32
BF16 = jnp.bfloat16


def iota(shape, dim):
    return lax.broadcasted_iota(jnp.int32, shape, dim)


def dot(a, b):
    return jnp.dot(a, b, preferred_element_type=F32)


def dot_t(a, b):
    return lax.dot_general(a, b, (((1,), (1,)), ((), ())), preferred_element_type=F32)


def one_hot(condition):
    return jnp.where(condition, 1.0, 0.0)


def norm_base(values):
    center = values - jnp.mean(values, axis=-1, keepdims=True)
    spread = jnp.mean(center * center, axis=-1, keepdims=True)
    return center * lax.rsqrt(spread + 1e-06)


def body(
    dims,
    enc_hbm,
    pairs_hbm,
    embed_hbm,
    gain_q_ref,
    gain_k_ref,
    gain_o_ref,
    wk_hbm,
    wv_hbm,
    wq_hbm,
    wo_hbm,
    head_hbm,
    out_ref,
    enc,
    pairs,
    embed,
    wqkv,
    wo,
    head,
    zs,
    zr,
    ys,
    yr,
    xs,
    xr,
    ns,
    nr,
    us,
    ur,
    bs,
    br,
    oout,
    in_sem,
    z_sem,
    y_sem,
    x_sem,
    n_sem,
    u_sem,
    b_sem,
    o_sem,
    w_send,
    w_recv,
):
    ny, nz, nc, tp, imgs, toks, tk, pairs_dev, pp, dm, gw, cols = dims
    nd = ny * nc
    half = nz // 2
    views = 2 * pairs_dev
    rows = tp * tk * 2 * pp
    chunks, width = zs.shape[0], zs.shape[3]
    slots = nz * tk * nd
    img = lax.axis_index("img")
    t = lax.axis_index("tp")
    c = lax.rem(img, nc)
    z = lax.rem(img // nc, nz)
    y = img // (nc * nz)
    d = y * nc + c

    def img_of(dd, zz):
        return (dd // nc) * (nz * nc) + zz * nc + lax.rem(dd, nc)

    sent = []

    class Send:
        def __init__(self, src, dst, send, recv, device):
            self.copy = pltpu.make_async_remote_copy(
                src_ref=src, dst_ref=dst, send_sem=send, recv_sem=recv, device_id=device, device_id_type=MESH
            )

        def start(self):
            self.copy.start()
            sent.append(self.copy)

        def wait_recv(self):
            self.copy.wait_recv()

    remote = Send

    loads = [
        pltpu.make_async_copy(src, dst, in_sem.at[i])
        for i, (src, dst) in enumerate(
            [
                (enc_hbm, enc),
                (embed_hbm, embed),
                (wk_hbm, wqkv.at[0, 0:gw]),
                (wv_hbm, wqkv.at[0, gw : 2 * gw]),
                (wq_hbm, wqkv.at[0, 2 * gw : 3 * gw]),
                (pairs_hbm, pairs),
                (wo_hbm, wo.at[0]),
                (head_hbm, head.at[t]),
            ]
        )
    ]
    for i in (5, 0, 1, 2, 3, 4, 6, 7):
        loads[i].start()

    barrier = pltpu.get_barrier_semaphore()
    far_first = [k for near in range(half, 0, -1) for k in sorted({near, nz - near})]
    partners = (
        [(img_of(d, lax.rem(z + k, nz)), t) for k in far_first]
        + [(img_of(lax.rem(d + r, nd), z), t) for r in range(1, nd)]
        + [(img, lax.rem(t + r, tp)) for r in range(1, tp)]
    )
    for partner in partners:
        pl.semaphore_signal(barrier, inc=1, device_id=partner, device_id_type=MESH)

    lanes = pairs.shape[2]
    z_par = lanes // (nc * pairs_dev)
    blocks_y = nz // z_par
    log_img = imgs.bit_length() - 1
    log_c = nc.bit_length() - 1
    log_z = nz.bit_length() - 1

    def parts_of(ids):
        owner = ids >> log_img
        return ids & (imgs - 1), owner & (nc - 1), (owner >> log_c) & (nz - 1), owner >> (log_c + log_z)

    def lane_parts(shape):
        lane = iota(shape, 1)
        return lane // (nc * pairs_dev), (lane // pairs_dev) % nc, lane % pairs_dev

    loads[5].wait()
    taken = jnp.zeros((pairs.shape[0], lanes), F32)
    for side in range(2):
        im, oc, oz, oy = parts_of(pairs[:, side, :])
        taken = taken + jnp.where((oc == c) & (oz == z) & (oy == y), im + 1, 0).astype(F32)
    row, col = iota((slots, pairs.shape[0]), 0), iota((slots, pairs.shape[0]), 1)
    block_of = (row % nd) // nc * blocks_y + ((z + row // (tk * nd)) & (nz - 1)) // z_par
    spread = dot(one_hot(col == block_of).astype(BF16), taken.astype(BF16))
    row = iota((slots, lanes), 0)
    lane_par, lane_core, _ = lane_parts((slots, lanes))
    keep = (lane_par == ((z + row // (tk * nd)) & (z_par - 1))) & (lane_core == row % nc)
    which = jnp.sum(jnp.where(keep, spread, 0.0), axis=1, keepdims=True)
    row, col = iota((slots, tk * imgs), 0), iota((slots, tk * imgs), 1)
    slot_hot = one_hot((which == (col % imgs + 1).astype(F32)) & (col // imgs == (row // nd) % tk))
    slot_mat = slot_hot.astype(BF16)

    row, col = iota((tk * imgs, imgs * toks), 0), iota((tk * imgs, imgs * toks), 1)
    pick = one_hot(col == row % imgs * toks + t * tk + row // imgs).astype(BF16)
    loads[0].wait()
    mine = dot(pick, enc[...]).astype(BF16)
    loads[1].wait()

    def send_z(src, dst, sem, h):
        out = []
        for k in far_first:
            copy = remote(
                src.at[h, k],
                dst.at[h, nz - k],
                sem.at[0, h, k],
                sem.at[1, h, k],
                (img_of(d, lax.rem(z + k, nz)), t),
            )
            copy.start()
            out.append(copy)
        dst[h, 0] = src[h, 0]
        return out

    def send_y(src, dst, sem, h):
        out = []
        for r in sorted(range(1, nd), key=lambda r: abs(2 * r - nd)):
            other = lax.rem(d + r, nd)
            copy = remote(
                src.at[h, other], dst.at[h, d], sem.at[0, h, r], sem.at[1, h, r], (img_of(other, z), t)
            )
            copy.start()
            out.append(copy)
        dst[h, d] = src[h, d]
        return out

    def send_x(src, dst, sem, h):
        out = []
        for r in sorted(range(1, tp), key=lambda r: abs(2 * r - tp)):
            other = lax.rem(t + r, tp)
            copy = remote(src.at[h, other], dst.at[h, t], sem.at[0, h, r], sem.at[1, h, r], (img, other))
            copy.start()
            out.append(copy)
        dst[h, t] = src[h, t]
        return out

    def wait_all(copies):
        for copy in copies:
            copy.wait_recv()

    z_copies = []
    for h in range(chunks):
        embedded = dot(mine, embed[:, h * width : (h + 1) * width]).astype(BF16)
        zs[h] = dot(slot_mat, embedded).astype(BF16).reshape(nz, tk * nd, width)
        if h == 0:
            pl.semaphore_wait(barrier, len(partners))
        z_copies.append(send_z(zs, zr, z_sem, h))

    next_t, prev_t = lax.rem(t + 1, tp), lax.rem(t + tp - 1, tp)
    far_t = lax.rem(t + 2, tp)
    sibling = (img_of(y * nc + (1 - c), z), t)

    def weight_copies(which, buf, own, before, after, far, own_after, own_before, far_slot):
        quarter = buf.shape[1] // 4

        def part(slot, u):
            return buf.at[slot, pl.ds(pl.multiple_of((2 * c + u) * quarter, quarter), quarter)]

        out = {}

        def add(name, src, dst, device):
            i = len(out)
            out[name] = remote(src, dst, w_send.at[which, i], w_recv.at[which, i], device)

        for u in range(2):
            add(("up", u), part(own, u), part(own_after, u), (img, next_t))
            add(("down", u), part(own, u), part(own_before, u), (img, prev_t))
        add("fwd_up", part(before, 0), part(far_slot, 0), (img, next_t))
        add("fwd_down", part(after, 1), part(far_slot, 1), (img, prev_t))
        for u in range(2):
            add(("sib_before", u), part(before, u), part(before, u), sibling)
            add(("sib_after", u), part(after, u), part(after, u), sibling)
            add(("sib_far", u), part(far, u), part(far, u), sibling)
        return out

    w_qkv = weight_copies(0, wqkv, 0, 3, 1, 2, 3, 1, 2)
    w_out = weight_copies(1, wo, 0, 3, 1, 2, 3, 1, 2)

    def head_part(slot, u):
        quarter = head.shape[1] // 4
        return head.at[slot, pl.ds(pl.multiple_of((2 * c + u) * quarter, quarter), quarter)]

    w_head = {}

    def add_head(name, slot, u, device):
        i = len(w_head)
        w_head[name] = remote(head_part(slot, u), head_part(slot, u), w_send.at[2, i], w_recv.at[2, i], device)

    for u in range(2):
        add_head(("up", u), t, u, (img, next_t))
        add_head(("down", u), t, u, (img, prev_t))
    add_head("fwd_up", prev_t, 0, (img, next_t))
    add_head("fwd_down", next_t, 1, (img, prev_t))
    for u in range(2):
        add_head(("sib_before", u), prev_t, u, sibling)
        add_head(("sib_after", u), next_t, u, sibling)
        add_head(("sib_far", u), far_t, u, sibling)

    def first_sends(w):
        for u in range(2):
            w["up", u].start()
            w["down", 1 - u].start()

    def pass_on(w, u):
        w["up", u].wait_recv()
        if u == 0:
            w["fwd_up"].start()
        w["sib_before", u].start()
        w["down", 1 - u].wait_recv()
        if u == 0:
            w["fwd_down"].start()
        w["sib_after", 1 - u].start()

    def pass_far(w):
        w["fwd_up"].wait_recv()
        w["sib_far", 0].start()
        w["fwd_down"].wait_recv()
        w["sib_far", 1].start()

    def arrive(w, name):
        for u in range(2):
            w[name, u].wait_recv()

    for i in (2, 3, 4):
        loads[i].wait()
    first_sends(w_qkv)
    loads[6].wait()
    first_sends(w_out)

    row, col = iota((slots, slots), 0), iota((slots, slots), 1)
    same_token = (row // nz) % tk == (col // nd) % tk
    turn_mat = one_hot((row % nz == col // (tk * nd)) & (row // (tk * nz) == col % nd) & same_token).astype(BF16)
    same_token = (row // nd) % tk == (col // nz) % tk
    turn_back = one_hot((row // (tk * nd) == col % nz) & (row % nd == col // (tk * nz)) & same_token).astype(BF16)

    both = pairs[y * blocks_y + z // z_par]
    lane_par, lane_core, lane_pair = lane_parts((1, lanes))
    at_me = (lane_par == lax.rem(z, z_par)) & (lane_core == c)
    slot_rows = iota((nd * nz, lanes), 0)
    view = iota((views, lanes), 0)
    view_pair = view // (2 * pp) * pp + view % pp
    view_side = (view // pp) % 2
    view_mat = jnp.zeros((views, nd * nz), F32)
    back_mat = jnp.zeros((nd * nz, views), F32)
    for side in range(2):
        im, oc, oz, oy = parts_of(both[side : side + 1])
        code = jnp.where(at_me, (oy * nc + oc) * nz + ((oz - z + nz) & (nz - 1)), -1)
        from_hot = one_hot(slot_rows == code).astype(BF16)
        view_hot = one_hot(at_me & (lane_pair == view_pair) & (view_side == side)).astype(BF16)
        view_mat = view_mat + dot_t(view_hot, from_hot)
        back_mat = back_mat + dot_t(from_hot, view_hot)
    view_mat = view_mat.astype(BF16)
    back_mat = back_mat.astype(BF16)
    sum_mat = slot_hot.T.astype(BF16)

    y_copies = []
    for h in range(chunks):
        if h == 0:
            pass_on(w_qkv, 0)
        elif h == chunks - 1:
            pass_on(w_qkv, 1)
            pass_on(w_out, 0)
            pass_on(w_out, 1)
        wait_all(z_copies[h])
        got = dot(turn_mat, zr[h].reshape(slots, width))
        ys[h] = got.astype(BF16).reshape(nd, tk, nz, width)
        y_copies.append(send_y(ys, yr, y_sem, h))
    pass_far(w_qkv)
    pass_far(w_out)

    x_copies = []
    for h in range(chunks):
        wait_all(y_copies[h])
        for ch in range(tk):
            got = dot(view_mat, yr[h, :, ch].reshape(nd * nz, width))
            xs[h, :, ch] = got.astype(BF16).reshape(tp, 2 * pp, width)
        x_copies.append(send_x(xs, xr, x_sem, h))

    loads[7].wait()
    first_sends(w_head)
    for h in range(chunks):
        wait_all(x_copies[h])

    x = jnp.concatenate([xr[h].reshape(rows, width) for h in range(chunks)], axis=1).astype(F32)
    base = norm_base(x)
    nq = (base * gain_q_ref[...].astype(F32).reshape(1, dm)).astype(BF16)
    nk = (base * gain_k_ref[...].astype(F32).reshape(1, dm)).astype(BF16)
    heads = gw // HEAD_DIM
    r0, r1 = iota((heads * rows, rows), 0) % rows, iota((heads * rows, rows), 1)
    seen = (r0 % pp == r1 % pp) & ((r0 // pp) % 2 != (r1 // pp) % 2)
    lane_head = iota((rows, gw), 1) // HEAD_DIM
    mixed = jnp.zeros((rows, dm), F32)
    for k, name in ((0, None), (3, "sib_before"), (1, "sib_after"), (2, "sib_far")):
        if name:
            arrive(w_qkv, name)
        keys = dot_t(nk, wqkv[k, 0:gw]).astype(BF16)
        values = dot_t(nk, wqkv[k, gw : 2 * gw]).astype(BF16)
        query = (dot_t(nq, wqkv[k, 2 * gw : 3 * gw]) * HEAD_DIM ** (-0.5)).astype(BF16)
        each = [jnp.where(lane_head == h, query, jnp.zeros_like(query)) for h in range(heads)]
        scores = jnp.where(seen, dot_t(jnp.concatenate(each, axis=0), keys), -1e38)
        raised = jnp.exp(scores - jnp.max(scores, axis=-1, keepdims=True))
        weights = raised * (1.0 / jnp.sum(raised, axis=-1, keepdims=True))
        found = dot(weights.astype(BF16), values)
        attended = found[0:rows]
        for h in range(1, heads):
            attended = jnp.where(lane_head == h, found[h * rows : (h + 1) * rows], attended)
        if name:
            arrive(w_out, name)
        mixed = mixed + dot(attended.astype(BF16), wo[k]).astype(BF16).astype(F32)
    normed = norm_base(x + mixed) * gain_o_ref[...].astype(F32).reshape(1, dm)
    for h in range(chunks):
        ns[h] = normed[:, h * width : (h + 1) * width].astype(BF16).reshape(tp, tk, 2 * pp, width)

    n_copies = [send_x(ns, nr, n_sem, h) for h in range(chunks)]
    u_copies = []
    for h in range(chunks):
        wait_all(n_copies[h])
        for ch in range(tk):
            got = dot(back_mat, nr[h, :, ch].reshape(views, width))
            us[h, :, ch] = got.astype(BF16).reshape(nd, nz, width)
        u_copies.append(send_y(us, ur, u_sem, h))
    b_copies = []
    for h in range(chunks):
        wait_all(u_copies[h])
        got = dot(turn_back, ur[h].reshape(slots, width))
        bs[h] = got.astype(BF16).reshape(nz, tk * nd, width)
        b_copies.append(send_z(bs, br, b_sem, h))

    pass_on(w_head, 0)
    pass_on(w_head, 1)
    pass_far(w_head)
    for name in ("sib_before", "sib_after", "sib_far"):
        arrive(w_head, name)

    maps = jnp.zeros((tk * imgs, tp * cols), F32)
    for h in range(chunks):
        wait_all(b_copies[h])
        summed = dot(sum_mat, br[h].reshape(slots, width)).astype(BF16)
        weight = head[...].reshape(dm, tp * cols)[h * width : (h + 1) * width]
        maps = maps + dot(summed, weight)
    maps = maps.astype(BF16)
    for r in range(tp):
        oout[r] = maps[:, r * cols : (r + 1) * cols].reshape(tk, imgs, cols)
    o_copies = []
    for r in sorted(range(1, tp), key=lambda r: abs(2 * r - tp)):
        other = lax.rem(t + r, tp)
        copy = remote(oout.at[other], out_ref.at[t], o_sem.at[0, r], o_sem.at[1, r], (img, other))
        copy.start()
        o_copies.append(copy)
    out_ref[t] = oout[t]
    wait_all(o_copies)

    for copy in sent:
        copy.wait_send()


def shards(
    encoded,
    pair_images,
    embed_w,
    gain_query,
    gain_key,
    gain_out,
    w_query,
    w_key,
    w_value,
    w_out,
    head_w,
):
    ny, nz, nc = GRID
    tp = lax.axis_size("tp")
    owners = lax.axis_size("img")
    imgs, toks, de = encoded.shape
    dm = embed_w.shape[1]
    gw = dm // tp
    tk = toks // tp
    pairs_dev = pair_images.shape[0] // owners
    pp = pairs_dev // tp
    cols = head_w.shape[1] // tp
    nd = ny * nc
    lanes = min(LANES, nz * nc * pairs_dev)
    blocks = pair_images.shape[0] // lanes
    pairs = pair_images.reshape(blocks, lanes, 2).transpose(0, 2, 1)
    dims = (ny, nz, nc, tp, imgs, toks, tk, pairs_dev, pp, dm, gw, cols)
    hbm = pl.BlockSpec(memory_space=pl.ANY)
    vmem = pl.BlockSpec(memory_space=pltpu.VMEM)
    dma = pltpu.SemaphoreType.DMA
    width = dm // CHUNKS
    swap_z = pltpu.VMEM((CHUNKS, nz, tk * nd, width), BF16)
    swap_y = pltpu.VMEM((CHUNKS, nd, tk, nz, width), BF16)
    swap_x = pltpu.VMEM((CHUNKS, tp, tk, 2 * pp, width), BF16)
    out = pl.pallas_call(
        functools.partial(body, dims),
        name="sublayer",
        out_shape=jax.ShapeDtypeStruct((tp, tk, imgs, cols), BF16),
        in_specs=[hbm] * 3 + [vmem] * 3 + [hbm] * 5,
        out_specs=vmem,
        scratch_shapes=[
            pltpu.VMEM((imgs * toks, de), BF16),
            pltpu.VMEM(pairs.shape, jnp.int32),
            pltpu.VMEM(embed_w.shape, BF16),
            pltpu.VMEM((tp, 3 * gw, dm), BF16),
            pltpu.VMEM((tp, gw, dm), BF16),
            pltpu.VMEM((tp, gw, tp * cols), BF16),
            swap_z,
            swap_z,
            swap_y,
            swap_y,
            swap_x,
            swap_x,
            swap_x,
            swap_x,
            swap_y,
            swap_y,
            swap_z,
            swap_z,
            pltpu.VMEM((tp, tk, imgs, cols), BF16),
            dma((8,)),
            dma((2, CHUNKS, nz)),
            dma((2, CHUNKS, nd)),
            dma((2, CHUNKS, tp)),
            dma((2, CHUNKS, tp)),
            dma((2, CHUNKS, nd)),
            dma((2, CHUNKS, nz)),
            dma((2, tp)),
            dma((3, 12)),
            dma((3, 12)),
        ],
        compiler_params=pltpu.CompilerParams(
            collective_id=0, has_side_effects=True, vmem_limit_bytes=63 * 1024 * 1024
        ),
    )(
        encoded.reshape(imgs * toks, de),
        pairs,
        embed_w,
        gain_query,
        gain_key,
        gain_out,
        w_key.T,
        w_value.T,
        w_query.T,
        w_out,
        head_w,
    )
    return out.reshape(toks, imgs, cols).transpose(1, 0, 2)


def solution(mesh):
    placed = (
        P("img", None, None),
        P(),
        P(),
        P(),
        P(),
        P(),
        P(None, "tp"),
        P(None, "tp"),
        P(None, "tp"),
        P("tp", None),
        P("tp", None),
    )
    return jax.shard_map(
        shards, mesh=mesh, in_specs=placed, out_specs=P("img", None, "tp"), check_vma=False
    )
```

time: 108 us -> 86.8 us (0.80); the launches traced: 106 us -> 86.6 us
  Pallas kernels: 95.7 us -> 85.1 us
  local copies, waits for them, and re-layouts: 10.7 us -> 1.49 us
    pallas_call x1, Pallas kernels: 95.7 us -> 85.1 us  [shards(): pl.pallas_call(functools.partial(body, dims), name='sublayer', out_shape=...]
    unnamed x16 -> x0, local copies, waits for them, and re-layouts: 7.95 us -> none
    another operation x3 -> x0, local copies, waits for them, and re-layouts: 2.05 us -> none  [shards(): gains = jnp.stack([gain_query, gain_key, gain_out]).astype(F32)]
where the time goes in v2:
time: 86.8 us; the launch traced here: 86.6 us
  Pallas kernels  85.1 us (98%)
  local copies, waits for them, and re-layouts  1.49 us (2%)
    pallas_call x1, Pallas kernels, shards(): pl.pallas_call(functools.partial(body, dims), name='sublayer', out_shape=...  85.1 us

profile of v2, /device:TPU:1, one launch (start us, length us, event | category | flops | bytes accessed | tf_op | source)
XLA Modules:
  0.0 86.6 jit_solution(17113992605247181919)
XLA Ops:
  0.0 85.1 %sublayer.1 = bf16[4,2,16,256]{3,2,1,0:T(8,128)(2,1)} custom-call(bf16[128,1024]{1,0:T(8,128)(2,1)} %bitcast.14, s32[32,2,128]{2,1,0:T(2,128)} %bitcast.16, bf16[1024,768]{1,0:T(8,128)(2,1)} %embed_hbm.1, bf16[768]{0:T(1024)(128)(2,1)} %gain_q_ref.1, bf16[768]{0:T(1024)(128)(2,1)} %gain_k_ref.1, bf16[768]{0:T(1024)(128)(2,1)} %gain_o_ref.1, ...), custom_call_target="tpu_custom_call" | custom-call | tf_op jit(solution)/shard_map/sublayer/pallas_call | solution.py:476
  85.1 1.5 %copy.14 = bf16[8,16,256]{2,0,1:T(8,128)(2,1)} copy(bf16[8,16,256]{2,1,0:T(8,128)(2,1)} %bitcast.15) | data formatting | bytes 131072 | tf_op jit(solution)/shard_map/reshape | solution.py:529

commit v3 on v2

--- a/solution.py
+++ b/solution.py
@@ -43,15 +43,18 @@
     enc_hbm,
     pairs_hbm,
     embed_hbm,
-    gain_q_ref,
-    gain_k_ref,
-    gain_o_ref,
+    gain_q_hbm,
+    gain_k_hbm,
+    gain_o_hbm,
     wk_hbm,
     wv_hbm,
     wq_hbm,
     wo_hbm,
     head_hbm,
     out_ref,
+    gain_q,
+    gain_k,
+    gain_o,
     enc,
     pairs,
     embed,
@@ -79,6 +82,7 @@
     u_sem,
     b_sem,
     o_sem,
+    o_own,
     w_send,
     w_recv,
 ):
@@ -92,12 +96,17 @@
     img = lax.axis_index("img")
     t = lax.axis_index("tp")
     c = lax.rem(img, nc)
-    z = lax.rem(img // nc, nz)
-    y = img // (nc * nz)
+    z = lax.rem(lax.div(img, nc), nz)
+    y = lax.div(img, nc * nz)
     d = y * nc + c
-
-    def img_of(dd, zz):
-        return (dd // nc) * (nz * nc) + zz * nc + lax.rem(dd, nc)
+    line = img - z * nc
+    plane = z * nc
+
+    def at_z_of(k):
+        return (line + lax.rem(z + k, nz) * nc, t)
+
+    def at_d_of(other):
+        return (plane + lax.div(other, nc) * (nz * nc) + lax.rem(other, nc), t)
 
     sent = []
 
@@ -109,12 +118,35 @@
 
         def start(self):
             self.copy.start()
-            sent.append(self.copy)
+            sent.append(self.copy.wait_send)
 
         def wait_recv(self):
             self.copy.wait_recv()
 
-    remote = Send
+    class Swap:
+        def __init__(self, src, dst, sem, here, pairs_of, own=None):
+            for there, place, device in pairs_of:
+                pltpu.make_async_remote_copy(
+                    src_ref=src.at[there],
+                    dst_ref=dst.at[place],
+                    send_sem=sem.at[0],
+                    recv_sem=sem.at[1],
+                    device_id=device,
+                    device_id_type=MESH,
+                ).start()
+            if own is None:
+                dst[here] = src[here]
+            else:
+                keep = pltpu.make_async_copy(src.at[here], dst.at[here], own)
+                keep.start()
+                sent.append(keep.wait)
+            some = pl.ds(0, len(pairs_of))
+            self.left = pltpu.make_async_copy(src.at[some], src.at[some], sem.at[0])
+            self.came = pltpu.make_async_copy(dst.at[some], dst.at[some], sem.at[1])
+            sent.append(self.left.wait)
+
+        def wait_recv(self):
+            self.came.wait()
 
     loads = [
         pltpu.make_async_copy(src, dst, in_sem.at[i])
@@ -128,20 +160,23 @@
                 (pairs_hbm, pairs),
                 (wo_hbm, wo.at[0]),
                 (head_hbm, head.at[t]),
+                (gain_q_hbm, gain_q),
+                (gain_k_hbm, gain_k),
+                (gain_o_hbm, gain_o),
             ]
         )
     ]
-    for i in (5, 0, 1, 2, 3, 4, 6, 7):
-        loads[i].start()
-
     barrier = pltpu.get_barrier_semaphore()
     far_first = [k for near in range(half, 0, -1) for k in sorted({near, nz - near})]
     partners = (
-        [(img_of(d, lax.rem(z + k, nz)), t) for k in far_first]
-        + [(img_of(lax.rem(d + r, nd), z), t) for r in range(1, nd)]
+        [at_z_of(k) for k in far_first]
+        + [at_d_of(lax.rem(d + r, nd)) for r in range(1, nd)]
         + [(img, lax.rem(t + r, tp)) for r in range(1, tp)]
     )
-    for partner in partners:
+    for i, partner in enumerate(partners):
+        if i == 5:
+            for first in (5, 0, 1):
+                loads[first].start()
         pl.semaphore_signal(barrier, inc=1, device_id=partner, device_id_type=MESH)
 
     lanes = pairs.shape[2]
@@ -180,47 +215,21 @@
     loads[0].wait()
     mine = dot(pick, enc[...]).astype(BF16)
     loads[1].wait()
+    for i in (2, 3, 4, 6, 7, 8, 9, 10):
+        loads[i].start()
 
     def send_z(src, dst, sem, h):
-        out = []
-        for k in far_first:
-            copy = remote(
-                src.at[h, k],
-                dst.at[h, nz - k],
-                sem.at[0, h, k],
-                sem.at[1, h, k],
-                (img_of(d, lax.rem(z + k, nz)), t),
-            )
-            copy.start()
-            out.append(copy)
-        dst[h, 0] = src[h, 0]
-        return out
+        return Swap(
+            src.at[h], dst.at[h], sem.at[h], 0, [(k, nz - k, at_z_of(k)) for k in far_first]
+        )
 
     def send_y(src, dst, sem, h):
-        out = []
-        for r in sorted(range(1, nd), key=lambda r: abs(2 * r - nd)):
-            other = lax.rem(d + r, nd)
-            copy = remote(
-                src.at[h, other], dst.at[h, d], sem.at[0, h, r], sem.at[1, h, r], (img_of(other, z), t)
-            )
-            copy.start()
-            out.append(copy)
-        dst[h, d] = src[h, d]
-        return out
+        others = [lax.rem(d + r, nd) for r in sorted(range(1, nd), key=lambda r: abs(2 * r - nd))]
+        return Swap(src.at[h], dst.at[h], sem.at[h], d, [(other, d, at_d_of(other)) for other in others])
 
     def send_x(src, dst, sem, h):
-        out = []
-        for r in sorted(range(1, tp), key=lambda r: abs(2 * r - tp)):
-            other = lax.rem(t + r, tp)
-            copy = remote(src.at[h, other], dst.at[h, t], sem.at[0, h, r], sem.at[1, h, r], (img, other))
-            copy.start()
-            out.append(copy)
-        dst[h, t] = src[h, t]
-        return out
-
-    def wait_all(copies):
-        for copy in copies:
-            copy.wait_recv()
+        others = [lax.rem(t + r, tp) for r in sorted(range(1, tp), key=lambda r: abs(2 * r - tp))]
+        return Swap(src.at[h], dst.at[h], sem.at[h], t, [(other, t, (img, other)) for other in others])
 
     z_copies = []
     for h in range(chunks):
@@ -232,78 +241,53 @@
 
     next_t, prev_t = lax.rem(t + 1, tp), lax.rem(t + tp - 1, tp)
     far_t = lax.rem(t + 2, tp)
-    sibling = (img_of(y * nc + (1 - c), z), t)
-
-    def weight_copies(which, buf, own, before, after, far, own_after, own_before, far_slot):
+    sibling = (img + 1 - 2 * c, t)
+
+    def weight_copies(which, buf, here, there_up, there_down, after, before, far_here, far_there):
         quarter = buf.shape[1] // 4
 
-        def part(slot, u):
-            return buf.at[slot, pl.ds(pl.multiple_of((2 * c + u) * quarter, quarter), quarter)]
-
-        out = {}
+        def part(slot, first, count):
+            start = (2 * c + first) * quarter
+            return buf.at[slot, pl.ds(pl.multiple_of(start, quarter), count * quarter)]
+
+        copies = {}
 
         def add(name, src, dst, device):
-            i = len(out)
-            out[name] = remote(src, dst, w_send.at[which, i], w_recv.at[which, i], device)
-
-        for u in range(2):
-            add(("up", u), part(own, u), part(own_after, u), (img, next_t))
-            add(("down", u), part(own, u), part(own_before, u), (img, prev_t))
-        add("fwd_up", part(before, 0), part(far_slot, 0), (img, next_t))
-        add("fwd_down", part(after, 1), part(far_slot, 1), (img, prev_t))
-        for u in range(2):
-            add(("sib_before", u), part(before, u), part(before, u), sibling)
-            add(("sib_after", u), part(after, u), part(after, u), sibling)
-            add(("sib_far", u), part(far, u), part(far, u), sibling)
-        return out
-
-    w_qkv = weight_copies(0, wqkv, 0, 3, 1, 2, 3, 1, 2)
-    w_out = weight_copies(1, wo, 0, 3, 1, 2, 3, 1, 2)
-
-    def head_part(slot, u):
-        quarter = head.shape[1] // 4
-        return head.at[slot, pl.ds(pl.multiple_of((2 * c + u) * quarter, quarter), quarter)]
-
-    w_head = {}
-
-    def add_head(name, slot, u, device):
-        i = len(w_head)
-        w_head[name] = remote(head_part(slot, u), head_part(slot, u), w_send.at[2, i], w_recv.at[2, i], device)
-
-    for u in range(2):
-        add_head(("up", u), t, u, (img, next_t))
-        add_head(("down", u), t, u, (img, prev_t))
-    add_head("fwd_up", prev_t, 0, (img, next_t))
-    add_head("fwd_down", next_t, 1, (img, prev_t))
-    for u in range(2):
-        add_head(("sib_before", u), prev_t, u, sibling)
-        add_head(("sib_after", u), next_t, u, sibling)
-        add_head(("sib_far", u), far_t, u, sibling)
+            i = len(copies)
+            copies[name] = Send(src, dst, w_send.at[which, i], w_recv.at[which, i], device)
+
+        add("up", part(here, 0, 2), part(there_up, 0, 2), (img, next_t))
+        add("down", part(here, 0, 2), part(there_down, 0, 2), (img, prev_t))
+        add("far_up", part(before, 0, 1), part(before if far_there is None else far_there, 0, 1), (img, next_t))
+        add("far_down", part(after, 1, 1), part(after if far_there is None else far_there, 1, 1), (img, prev_t))
+        add("before", part(before, 0, 2), part(before, 0, 2), sibling)
+        add("after", part(after, 0, 2), part(after, 0, 2), sibling)
+        add("far", part(far_here, 0, 2), part(far_here, 0, 2), sibling)
+        return copies
+
+    w_qkv = weight_copies(0, wqkv, 0, 3, 1, 1, 3, 2, 2)
+    w_out = weight_copies(1, wo, 0, 3, 1, 1, 3, 2, 2)
+    w_head = weight_copies(2, head, t, t, t, next_t, prev_t, far_t, None)
 
     def first_sends(w):
-        for u in range(2):
-            w["up", u].start()
-            w["down", 1 - u].start()
-
-    def pass_on(w, u):
-        w["up", u].wait_recv()
-        if u == 0:
-            w["fwd_up"].start()
-        w["sib_before", u].start()
-        w["down", 1 - u].wait_recv()
-        if u == 0:
-            w["fwd_down"].start()
-        w["sib_after", 1 - u].start()
+        w["up"].start()
+        w["down"].start()
+
+    def pass_on(w):
+        w["up"].wait_recv()
+        w["far_up"].start()
+        w["down"].wait_recv()
+        w["far_down"].start()
+        w["before"].start()
+        w["after"].start()
 
     def pass_far(w):
-        w["fwd_up"].wait_recv()
-        w["sib_far", 0].start()
-        w["fwd_down"].wait_recv()
-        w["sib_far", 1].start()
+        w["far_up"].wait_recv()
+        w["far_down"].wait_recv()
+        w["far"].start()
 
     def arrive(w, name):
-        for u in range(2):
-            w[name, u].wait_recv()
+        w[name].wait_recv()
 
     for i in (2, 3, 4):
         loads[i].wait()
@@ -339,42 +323,42 @@
 
     y_copies = []
     for h in range(chunks):
-        if h == 0:
-            pass_on(w_qkv, 0)
-        elif h == chunks - 1:
-            pass_on(w_qkv, 1)
-            pass_on(w_out, 0)
-            pass_on(w_out, 1)
-        wait_all(z_copies[h])
+        if h == chunks - 1:
+            pass_on(w_qkv)
+            pass_on(w_out)
+        z_copies[h].wait_recv()
         got = dot(turn_mat, zr[h].reshape(slots, width))
         ys[h] = got.astype(BF16).reshape(nd, tk, nz, width)
         y_copies.append(send_y(ys, yr, y_sem, h))
     pass_far(w_qkv)
-    pass_far(w_out)
 
     x_copies = []
     for h in range(chunks):
-        wait_all(y_copies[h])
+        y_copies[h].wait_recv()
         for ch in range(tk):
             got = dot(view_mat, yr[h, :, ch].reshape(nd * nz, width))
             xs[h, :, ch] = got.astype(BF16).reshape(tp, 2 * pp, width)
         x_copies.append(send_x(xs, xr, x_sem, h))
 
+    pass_far(w_out)
     loads[7].wait()
     first_sends(w_head)
     for h in range(chunks):
-        wait_all(x_copies[h])
+        x_copies[h].wait_recv()
+
+    for i in (8, 9, 10):
+        loads[i].wait()
 
     x = jnp.concatenate([xr[h].reshape(rows, width) for h in range(chunks)], axis=1).astype(F32)
     base = norm_base(x)
-    nq = (base * gain_q_ref[...].astype(F32).reshape(1, dm)).astype(BF16)
-    nk = (base * gain_k_ref[...].astype(F32).reshape(1, dm)).astype(BF16)
+    nq = (base * gain_q[...].astype(F32).reshape(1, dm)).astype(BF16)
+    nk = (base * gain_k[...].astype(F32).reshape(1, dm)).astype(BF16)
     heads = gw // HEAD_DIM
     r0, r1 = iota((heads * rows, rows), 0) % rows, iota((heads * rows, rows), 1)
     seen = (r0 % pp == r1 % pp) & ((r0 // pp) % 2 != (r1 // pp) % 2)
     lane_head = iota((rows, gw), 1) // HEAD_DIM
     mixed = jnp.zeros((rows, dm), F32)
-    for k, name in ((0, None), (3, "sib_before"), (1, "sib_after"), (2, "sib_far")):
+    for k, name in ((0, None), (3, "before"), (1, "after"), (2, "far")):
         if name:
             arrive(w_qkv, name)
         keys = dot_t(nk, wqkv[k, 0:gw]).astype(BF16)
@@ -391,51 +375,44 @@
         if name:
             arrive(w_out, name)
         mixed = mixed + dot(attended.astype(BF16), wo[k]).astype(BF16).astype(F32)
-    normed = norm_base(x + mixed) * gain_o_ref[...].astype(F32).reshape(1, dm)
+    normed = norm_base(x + mixed) * gain_o[...].astype(F32).reshape(1, dm)
     for h in range(chunks):
         ns[h] = normed[:, h * width : (h + 1) * width].astype(BF16).reshape(tp, tk, 2 * pp, width)
 
     n_copies = [send_x(ns, nr, n_sem, h) for h in range(chunks)]
     u_copies = []
     for h in range(chunks):
-        wait_all(n_copies[h])
+        n_copies[h].wait_recv()
         for ch in range(tk):
             got = dot(back_mat, nr[h, :, ch].reshape(views, width))
             us[h, :, ch] = got.astype(BF16).reshape(nd, nz, width)
         u_copies.append(send_y(us, ur, u_sem, h))
     b_copies = []
     for h in range(chunks):
-        wait_all(u_copies[h])
+        u_copies[h].wait_recv()
         got = dot(turn_back, ur[h].reshape(slots, width))
         bs[h] = got.astype(BF16).reshape(nz, tk * nd, width)
         b_copies.append(send_z(bs, br, b_sem, h))
 
-    pass_on(w_head, 0)
-    pass_on(w_head, 1)
+    pass_on(w_head)
     pass_far(w_head)
-    for name in ("sib_before", "sib_after", "sib_far"):
+    for name in ("before", "after", "far"):
         arrive(w_head, name)
 
     maps = jnp.zeros((tk * imgs, tp * cols), F32)
     for h in range(chunks):
-        wait_all(b_copies[h])
+        b_copies[h].wait_recv()
         summed = dot(sum_mat, br[h].reshape(slots, width)).astype(BF16)
         weight = head[...].reshape(dm, tp * cols)[h * width : (h + 1) * width]
         maps = maps + dot(summed, weight)
     maps = maps.astype(BF16)
     for r in range(tp):
         oout[r] = maps[:, r * cols : (r + 1) * cols].reshape(tk, imgs, cols)
-    o_copies = []
-    for r in sorted(range(1, tp), key=lambda r: abs(2 * r - tp)):
-        other = lax.rem(t + r, tp)
-        copy = remote(oout.at[other], out_ref.at[t], o_sem.at[0, r], o_sem.at[1, r], (img, other))
-        copy.start()
-        o_copies.append(copy)
-    out_ref[t] = oout[t]
-    wait_all(o_copies)
-
-    for copy in sent:
-        copy.wait_send()
+    others = [lax.rem(t + r, tp) for r in sorted(range(1, tp), key=lambda r: abs(2 * r - tp))]
+    Swap(oout, out_ref, o_sem, t, [(other, t, (img, other)) for other in others], o_own).wait_recv()
+
+    for wait in sent:
+        wait()
 
 
 def shards(
@@ -467,7 +444,6 @@
     pairs = pair_images.reshape(blocks, lanes, 2).transpose(0, 2, 1)
     dims = (ny, nz, nc, tp, imgs, toks, tk, pairs_dev, pp, dm, gw, cols)
     hbm = pl.BlockSpec(memory_space=pl.ANY)
-    vmem = pl.BlockSpec(memory_space=pltpu.VMEM)
     dma = pltpu.SemaphoreType.DMA
     width = dm // CHUNKS
     swap_z = pltpu.VMEM((CHUNKS, nz, tk * nd, width), BF16)
@@ -477,9 +453,12 @@
         functools.partial(body, dims),
         name="sublayer",
         out_shape=jax.ShapeDtypeStruct((tp, tk, imgs, cols), BF16),
-        in_specs=[hbm] * 3 + [vmem] * 3 + [hbm] * 5,
-        out_specs=vmem,
+        in_specs=[hbm] * 11,
+        out_specs=hbm,
         scratch_shapes=[
+            pltpu.VMEM((dm,), BF16),
+            pltpu.VMEM((dm,), BF16),
+            pltpu.VMEM((dm,), BF16),
             pltpu.VMEM((imgs * toks, de), BF16),
             pltpu.VMEM(pairs.shape, jnp.int32),
             pltpu.VMEM(embed_w.shape, BF16),
@@ -499,16 +478,17 @@
             swap_z,
             swap_z,
             pltpu.VMEM((tp, tk, imgs, cols), BF16),
-            dma((8,)),
-            dma((2, CHUNKS, nz)),
-            dma((2, CHUNKS, nd)),
-            dma((2, CHUNKS, tp)),
-            dma((2, CHUNKS, tp)),
-            dma((2, CHUNKS, nd)),
-            dma((2, CHUNKS, nz)),
-            dma((2, tp)),
-            dma((3, 12)),
-            dma((3, 12)),
+            dma((11,)),
+            dma((CHUNKS, 2)),
+            dma((CHUNKS, 2)),
+            dma((CHUNKS, 2)),
+            dma((CHUNKS, 2)),
+            dma((CHUNKS, 2)),
+            dma((CHUNKS, 2)),
+            dma((2,)),
+            dma,
+            dma((3, 7)),
+            dma((3, 7)),
         ],
         compiler_params=pltpu.CompilerParams(
             collective_id=0, has_side_effects=True, vmem_limit_bytes=63 * 1024 * 1024

time: 86.8 us -> 83.5 us (0.962)
  Pallas kernels: 85.1 us -> 81.5 us
    pallas_call x1, Pallas kernels: 85.1 us -> 81.5 us  [shards(): pl.pallas_call(functools.partial(body, dims), name='sublayer', out_shape=...]
where the time goes in v3:
time: 83.5 us; the launch traced here: 83 us
  Pallas kernels  81.5 us (98%)
  local copies, waits for them, and re-layouts  1.49 us (2%)
    pallas_call x1, Pallas kernels, shards(): pl.pallas_call(functools.partial(body, dims), name='sublayer', out_shape=...  81.5 us

profile of v3, /device:TPU:1, one launch (start us, length us, event | category | flops | bytes accessed | tf_op | source)
XLA Modules:
  0.0 83.0 jit_solution(8395929666036973279)
XLA Ops:
  0.0 81.5 %sublayer.1 = bf16[4,2,16,256]{3,2,1,0:T(8,128)(2,1)} custom-call(bf16[128,1024]{1,0:T(8,128)(2,1)} %bitcast.14, s32[32,2,128]{2,1,0:T(2,128)} %bitcast.16, bf16[1024,768]{1,0:T(8,128)(2,1)} %embed_hbm.1, bf16[768]{0:T(1024)(128)(2,1)} %gain_q_hbm.1, bf16[768]{0:T(1024)(128)(2,1)} %gain_k_hbm.1, bf16[768]{0:T(1024)(128)(2,1)} %gain_o_hbm.1, ...), custom_call_target="tpu_custom_call" | custom-call | tf_op jit(solution)/shard_map/sublayer/pallas_call | solution.py:452
  81.6 1.5 %copy.14 = bf16[8,16,256]{2,0,1:T(8,128)(2,1)} copy(bf16[8,16,256]{2,1,0:T(8,128)(2,1)} %bitcast.15) | data formatting | bytes 131072 | tf_op jit(solution)/shard_map/reshape | solution.py:509

commit v4 on v3

--- a/solution.py
+++ b/solution.py
@@ -10,7 +10,8 @@
 HEAD_DIM = 64
 GRID = (4, 16, 2)
 LANES = 128
-CHUNKS = 2
+FORWARD = (512, 256)
+BACK = (256, 512)
 MESH = pl.DeviceIdType.MESH
 F32 = jnp.float32
 BF16 = jnp.bfloat16
@@ -83,6 +84,7 @@
     b_sem,
     o_sem,
     o_own,
+    far_sem,
     w_send,
     w_recv,
 ):
@@ -91,7 +93,8 @@
     half = nz // 2
     views = 2 * pairs_dev
     rows = tp * tk * 2 * pp
-    chunks, width = zs.shape[0], zs.shape[3]
+    going = [(h, sum(FORWARD[:h]), width) for h, width in enumerate(FORWARD)]
+    coming = [(h, sum(BACK[:h]), width) for h, width in enumerate(BACK)]
     slots = nz * tk * nd
     img = lax.axis_index("img")
     t = lax.axis_index("tp")
@@ -124,26 +127,30 @@
             self.copy.wait_recv()
 
     class Swap:
-        def __init__(self, src, dst, sem, here, pairs_of, own=None):
-            for there, place, device in pairs_of:
-                pltpu.make_async_remote_copy(
-                    src_ref=src.at[there],
-                    dst_ref=dst.at[place],
-                    send_sem=sem.at[0],
-                    recv_sem=sem.at[1],
-                    device_id=device,
-                    device_id_type=MESH,
-                ).start()
+        def __init__(self, src, dst, sem, here, pairs_of, own=None, more=()):
+            self.src, self.dst, self.sem = src, dst, sem
+            self.start(pairs_of)
             if own is None:
                 dst[here] = src[here]
             else:
                 keep = pltpu.make_async_copy(src.at[here], dst.at[here], own)
                 keep.start()
                 sent.append(keep.wait)
-            some = pl.ds(0, len(pairs_of))
+            some = pl.ds(0, len(pairs_of) + len(more))
             self.left = pltpu.make_async_copy(src.at[some], src.at[some], sem.at[0])
             self.came = pltpu.make_async_copy(dst.at[some], dst.at[some], sem.at[1])
             sent.append(self.left.wait)
+
+        def start(self, pairs_of):
+            for there, place, device in pairs_of:
+                pltpu.make_async_remote_copy(
+                    src_ref=self.src.at[there],
+                    dst_ref=self.dst.at[place],
+                    send_sem=self.sem.at[0],
+                    recv_sem=self.sem.at[1],
+                    device_id=device,
+                    device_id_type=MESH,
+                ).start()
 
         def wait_recv(self):
             self.came.wait()
@@ -168,8 +175,11 @@
     ]
     barrier = pltpu.get_barrier_semaphore()
     far_first = [k for near in range(half, 0, -1) for k in sorted({near, nz - near})]
+    reach = half // 2
+    near = [k for k in far_first if min(k, nz - k) <= reach]
+    far = [k for k in far_first if min(k, nz - k) > reach]
     partners = (
-        [at_z_of(k) for k in far_first]
+        [at_z_of(k) for k in near]
         + [at_d_of(lax.rem(d + r, nd)) for r in range(1, nd)]
         + [(img, lax.rem(t + r, tp)) for r in range(1, tp)]
     )
@@ -218,26 +228,32 @@
     for i in (2, 3, 4, 6, 7, 8, 9, 10):
         loads[i].start()
 
-    def send_z(src, dst, sem, h):
-        return Swap(
-            src.at[h], dst.at[h], sem.at[h], 0, [(k, nz - k, at_z_of(k)) for k in far_first]
-        )
+    def z_places(some):
+        return [(k, nz - k, at_z_of(k)) for k in some]
+
+    def send_z(src, dst, sem, h, now, later):
+        return Swap(src[h], dst[h], sem.at[h], 0, z_places(now), more=later)
 
     def send_y(src, dst, sem, h):
         others = [lax.rem(d + r, nd) for r in sorted(range(1, nd), key=lambda r: abs(2 * r - nd))]
-        return Swap(src.at[h], dst.at[h], sem.at[h], d, [(other, d, at_d_of(other)) for other in others])
+        return Swap(src[h], dst[h], sem.at[h], d, [(other, d, at_d_of(other)) for other in others])
 
     def send_x(src, dst, sem, h):
         others = [lax.rem(t + r, tp) for r in sorted(range(1, tp), key=lambda r: abs(2 * r - tp))]
-        return Swap(src.at[h], dst.at[h], sem.at[h], t, [(other, t, (img, other)) for other in others])
+        return Swap(src[h], dst[h], sem.at[h], t, [(other, t, (img, other)) for other in others])
 
     z_copies = []
-    for h in range(chunks):
-        embedded = dot(mine, embed[:, h * width : (h + 1) * width]).astype(BF16)
-        zs[h] = dot(slot_mat, embedded).astype(BF16).reshape(nz, tk * nd, width)
+    for h, start, width in going:
+        embedded = dot(mine, embed[:, start : start + width]).astype(BF16)
+        zs[h][...] = dot(slot_mat, embedded).astype(BF16).reshape(nz, tk * nd, width)
         if h == 0:
             pl.semaphore_wait(barrier, len(partners))
-        z_copies.append(send_z(zs, zr, z_sem, h))
+            for k in (reach, nz - reach):
+                pl.semaphore_signal(far_sem, inc=1, device_id=at_z_of(k), device_id_type=MESH)
+        z_copies.append(send_z(zs, zr, z_sem, h, near, far))
+        if h == 0:
+            pl.semaphore_wait(far_sem, 2)
+        z_copies[h].start(z_places(far))
 
     next_t, prev_t = lax.rem(t + 1, tp), lax.rem(t + tp - 1, tp)
     far_t = lax.rem(t + 2, tp)
@@ -322,34 +338,34 @@
     sum_mat = slot_hot.T.astype(BF16)
 
     y_copies = []
-    for h in range(chunks):
-        if h == chunks - 1:
+    for h, start, width in going:
+        if h == len(going) - 1:
             pass_on(w_qkv)
             pass_on(w_out)
         z_copies[h].wait_recv()
-        got = dot(turn_mat, zr[h].reshape(slots, width))
-        ys[h] = got.astype(BF16).reshape(nd, tk, nz, width)
+        got = dot(turn_mat, zr[h][...].reshape(slots, width))
+        ys[h][...] = got.astype(BF16).reshape(nd, tk, nz, width)
         y_copies.append(send_y(ys, yr, y_sem, h))
     pass_far(w_qkv)
 
     x_copies = []
-    for h in range(chunks):
+    for h, start, width in going:
         y_copies[h].wait_recv()
         for ch in range(tk):
-            got = dot(view_mat, yr[h, :, ch].reshape(nd * nz, width))
-            xs[h, :, ch] = got.astype(BF16).reshape(tp, 2 * pp, width)
+            got = dot(view_mat, yr[h][:, ch].reshape(nd * nz, width))
+            xs[h][:, ch] = got.astype(BF16).reshape(tp, 2 * pp, width)
         x_copies.append(send_x(xs, xr, x_sem, h))
 
     pass_far(w_out)
     loads[7].wait()
     first_sends(w_head)
-    for h in range(chunks):
+    for h in range(len(going)):
         x_copies[h].wait_recv()
 
     for i in (8, 9, 10):
         loads[i].wait()
 
-    x = jnp.concatenate([xr[h].reshape(rows, width) for h in range(chunks)], axis=1).astype(F32)
+    x = jnp.concatenate([xr[h][...].reshape(rows, width) for h, _, width in going], axis=1).astype(F32)
     base = norm_base(x)
     nq = (base * gain_q[...].astype(F32).reshape(1, dm)).astype(BF16)
     nk = (base * gain_k[...].astype(F32).reshape(1, dm)).astype(BF16)
@@ -376,23 +392,23 @@
             arrive(w_out, name)
         mixed = mixed + dot(attended.astype(BF16), wo[k]).astype(BF16).astype(F32)
     normed = norm_base(x + mixed) * gain_o[...].astype(F32).reshape(1, dm)
-    for h in range(chunks):
-        ns[h] = normed[:, h * width : (h + 1) * width].astype(BF16).reshape(tp, tk, 2 * pp, width)
-
-    n_copies = [send_x(ns, nr, n_sem, h) for h in range(chunks)]
+    for h, start, width in coming:
+        ns[h][...] = normed[:, start : start + width].astype(BF16).reshape(tp, tk, 2 * pp, width)
+
+    n_copies = [send_x(ns, nr, n_sem, h) for h in range(len(coming))]
     u_copies = []
-    for h in range(chunks):
+    for h, start, width in coming:
         n_copies[h].wait_recv()
         for ch in range(tk):
-            got = dot(back_mat, nr[h, :, ch].reshape(views, width))
-            us[h, :, ch] = got.astype(BF16).reshape(nd, nz, width)
+            got = dot(back_mat, nr[h][:, ch].reshape(views, width))
+            us[h][:, ch] = got.astype(BF16).reshape(nd, nz, width)
         u_copies.append(send_y(us, ur, u_sem, h))
     b_copies = []
-    for h in range(chunks):
+    for h, start, width in coming:
         u_copies[h].wait_recv()
-        got = dot(turn_back, ur[h].reshape(slots, width))
-        bs[h] = got.astype(BF16).reshape(nz, tk * nd, width)
-        b_copies.append(send_z(bs, br, b_sem, h))
+        got = dot(turn_back, ur[h][...].reshape(slots, width))
+        bs[h][...] = got.astype(BF16).reshape(nz, tk * nd, width)
+        b_copies.append(send_z(bs, br, b_sem, h, far_first, ()))
 
     pass_on(w_head)
     pass_far(w_head)
@@ -400,10 +416,10 @@
         arrive(w_head, name)
 
     maps = jnp.zeros((tk * imgs, tp * cols), F32)
-    for h in range(chunks):
+    for h, start, width in coming:
         b_copies[h].wait_recv()
-        summed = dot(sum_mat, br[h].reshape(slots, width)).astype(BF16)
-        weight = head[...].reshape(dm, tp * cols)[h * width : (h + 1) * width]
+        summed = dot(sum_mat, br[h][...].reshape(slots, width)).astype(BF16)
+        weight = head[...].reshape(dm, tp * cols)[start : start + width]
         maps = maps + dot(summed, weight)
     maps = maps.astype(BF16)
     for r in range(tp):
@@ -445,10 +461,12 @@
     dims = (ny, nz, nc, tp, imgs, toks, tk, pairs_dev, pp, dm, gw, cols)
     hbm = pl.BlockSpec(memory_space=pl.ANY)
     dma = pltpu.SemaphoreType.DMA
-    width = dm // CHUNKS
-    swap_z = pltpu.VMEM((CHUNKS, nz, tk * nd, width), BF16)
-    swap_y = pltpu.VMEM((CHUNKS, nd, tk, nz, width), BF16)
-    swap_x = pltpu.VMEM((CHUNKS, tp, tk, 2 * pp, width), BF16)
+    def buffers(widths, *shape):
+        return tuple(pltpu.VMEM((*shape, width), BF16) for width in widths)
+
+    swap_z = nz, tk * nd
+    swap_y = nd, tk, nz
+    swap_x = tp, tk, 2 * pp
     out = pl.pallas_call(
         functools.partial(body, dims),
         name="sublayer",
@@ -465,28 +483,29 @@
             pltpu.VMEM((tp, 3 * gw, dm), BF16),
             pltpu.VMEM((tp, gw, dm), BF16),
             pltpu.VMEM((tp, gw, tp * cols), BF16),
-            swap_z,
-            swap_z,
-            swap_y,
-            swap_y,
-            swap_x,
-            swap_x,
-            swap_x,
-            swap_x,
-            swap_y,
-            swap_y,
-            swap_z,
-            swap_z,
+            buffers(FORWARD, *swap_z),
+            buffers(FORWARD, *swap_z),
+            buffers(FORWARD, *swap_y),
+            buffers(FORWARD, *swap_y),
+            buffers(FORWARD, *swap_x),
+            buffers(FORWARD, *swap_x),
+            buffers(BACK, *swap_x),
+            buffers(BACK, *swap_x),
+            buffers(BACK, *swap_y),
+            buffers(BACK, *swap_y),
+            buffers(BACK, *swap_z),
+            buffers(BACK, *swap_z),
             pltpu.VMEM((tp, tk, imgs, cols), BF16),
             dma((11,)),
-            dma((CHUNKS, 2)),
-            dma((CHUNKS, 2)),
-            dma((CHUNKS, 2)),
-            dma((CHUNKS, 2)),
-            dma((CHUNKS, 2)),
-            dma((CHUNKS, 2)),
+            dma((len(FORWARD), 2)),
+            dma((len(FORWARD), 2)),
+            dma((len(FORWARD), 2)),
+            dma((len(BACK), 2)),
+            dma((len(BACK), 2)),
+            dma((len(BACK), 2)),
             dma((2,)),
             dma,
+            pltpu.SemaphoreType.REGULAR,
             dma((3, 7)),
             dma((3, 7)),
         ],

time: 83.5 us -> 81.2 us (0.972)
  Pallas kernels: 81.5 us -> 79.5 us
    pallas_call x1, Pallas kernels: 81.5 us -> 79.5 us  [shards(): pl.pallas_call(functools.partial(body, dims), name='sublayer', out_shape=...]
where the time goes in v4:
time: 81.2 us; the launch traced here: 81 us
  Pallas kernels  79.5 us (98%)
  local copies, waits for them, and re-layouts  1.49 us (2%)
    pallas_call x1, Pallas kernels, shards(): pl.pallas_call(functools.partial(body, dims), name='sublayer', out_shape=...  79.5 us

profile of v4, /device:TPU:1, one launch (start us, length us, event | category | flops | bytes accessed | tf_op | source)
XLA Modules:
  0.0 81.0 jit_solution(14640606800363791843)
XLA Ops:
  0.0 79.5 %sublayer.1 = bf16[4,2,16,256]{3,2,1,0:T(8,128)(2,1)} custom-call(bf16[128,1024]{1,0:T(8,128)(2,1)} %bitcast.14, s32[32,2,128]{2,1,0:T(2,128)} %bitcast.16, bf16[1024,768]{1,0:T(8,128)(2,1)} %embed_hbm.1, bf16[768]{0:T(1024)(128)(2,1)} %gain_q_hbm.1, bf16[768]{0:T(1024)(128)(2,1)} %gain_k_hbm.1, bf16[768]{0:T(1024)(128)(2,1)} %gain_o_hbm.1, ...), custom_call_target="tpu_custom_call" | custom-call | tf_op jit(solution)/shard_map/sublayer/pallas_call | solution.py:470
  79.5 1.5 %copy.14 = bf16[8,16,256]{2,0,1:T(8,128)(2,1)} copy(bf16[8,16,256]{2,1,0:T(8,128)(2,1)} %bitcast.15) | data formatting | bytes 131072 | tf_op jit(solution)/shard_map/reshape | solution.py:528

commit v5 on v4

--- a/solution.py
+++ b/solution.py
@@ -59,6 +59,7 @@
     enc,
     pairs,
     embed,
+    raw,
     wqkv,
     wo,
     head,
@@ -161,9 +162,9 @@
             [
                 (enc_hbm, enc),
                 (embed_hbm, embed),
-                (wk_hbm, wqkv.at[0, 0:gw]),
-                (wv_hbm, wqkv.at[0, gw : 2 * gw]),
-                (wq_hbm, wqkv.at[0, 2 * gw : 3 * gw]),
+                (wk_hbm, raw.at[0:gw]),
+                (wv_hbm, raw.at[gw : 2 * gw]),
+                (wq_hbm, raw.at[2 * gw : 3 * gw]),
                 (pairs_hbm, pairs),
                 (wo_hbm, wo.at[0]),
                 (head_hbm, head.at[t]),
@@ -185,7 +186,7 @@
     )
     for i, partner in enumerate(partners):
         if i == 5:
-            for first in (5, 0, 1):
+            for first in (5, 0, 1, 2, 3, 4):
                 loads[first].start()
         pl.semaphore_signal(barrier, inc=1, device_id=partner, device_id_type=MESH)
 
@@ -225,7 +226,7 @@
     loads[0].wait()
     mine = dot(pick, enc[...]).astype(BF16)
     loads[1].wait()
-    for i in (2, 3, 4, 6, 7, 8, 9, 10):
+    for i in (6, 7, 8, 9, 10):
         loads[i].start()
 
     def z_places(some):
@@ -242,6 +243,60 @@
         others = [lax.rem(t + r, tp) for r in sorted(range(1, tp), key=lambda r: abs(2 * r - tp))]
         return Swap(src[h], dst[h], sem.at[h], t, [(other, t, (img, other)) for other in others])
 
+    next_t, prev_t = lax.rem(t + 1, tp), lax.rem(t + tp - 1, tp)
+    far_t = lax.rem(t + 2, tp)
+    sibling = (img + 1 - 2 * c, t)
+
+    def weight_copies(which, buf, here, there_up, there_down, after, before, far_here, far_there):
+        quarter = buf.shape[1] // 4
+
+        def part(slot, first, count):
+            start = (2 * c + first) * quarter
+            return buf.at[slot, pl.ds(pl.multiple_of(start, quarter), count * quarter)]
+
+        copies = {}
+
+        def add(name, src, dst, device):
+            i = len(copies)
+            copies[name] = Send(src, dst, w_send.at[which, i], w_recv.at[which, i], device)
+
+        add("up", part(here, 0, 2), part(there_up, 0, 2), (img, next_t))
+        add("down", part(here, 0, 2), part(there_down, 0, 2), (img, prev_t))
+        add("far_up", part(before, 0, 1), part(before if far_there is None else far_there, 0, 1), (img, next_t))
+        add("far_down", part(after, 1, 1), part(after if far_there is None else far_there, 1, 1), (img, prev_t))
+        add("before", part(before, 0, 2), part(before, 0, 2), sibling)
+        add("after", part(after, 0, 2), part(after, 0, 2), sibling)
+        add("far", part(far_here, 0, 2), part(far_here, 0, 2), sibling)
+        return copies
+
+    w_qkv = weight_copies(0, wqkv, 0, 3, 1, 1, 3, 2, 2)
+    w_out = weight_copies(1, wo, 0, 3, 1, 1, 3, 2, 2)
+    w_head = weight_copies(2, head, t, t, t, next_t, prev_t, far_t, None)
+
+    def first_sends(w):
+        w["up"].start()
+        w["down"].start()
+
+    def pass_on(w):
+        w["up"].wait_recv()
+        w["far_up"].start()
+        w["down"].wait_recv()
+        w["far_down"].start()
+        w["before"].start()
+        w["after"].start()
+
+    def pass_far(w):
+        w["far_up"].wait_recv()
+        w["far_down"].wait_recv()
+        w["far"].start()
+
+    def arrive(w, name):
+        w[name].wait_recv()
+
+    raw[3 * gw :] = jnp.zeros((raw.shape[0] - 3 * gw, dm), BF16)
+    for i in (2, 3, 4):
+        loads[i].wait()
+    wqkv[0] = raw[...].T
     z_copies = []
     for h, start, width in going:
         embedded = dot(mine, embed[:, start : start + width]).astype(BF16)
@@ -250,64 +305,12 @@
             pl.semaphore_wait(barrier, len(partners))
             for k in (reach, nz - reach):
                 pl.semaphore_signal(far_sem, inc=1, device_id=at_z_of(k), device_id_type=MESH)
+            first_sends(w_qkv)
         z_copies.append(send_z(zs, zr, z_sem, h, near, far))
         if h == 0:
             pl.semaphore_wait(far_sem, 2)
         z_copies[h].start(z_places(far))
 
-    next_t, prev_t = lax.rem(t + 1, tp), lax.rem(t + tp - 1, tp)
-    far_t = lax.rem(t + 2, tp)
-    sibling = (img + 1 - 2 * c, t)
-
-    def weight_copies(which, buf, here, there_up, there_down, after, before, far_here, far_there):
-        quarter = buf.shape[1] // 4
-
-        def part(slot, first, count):
-            start = (2 * c + first) * quarter
-            return buf.at[slot, pl.ds(pl.multiple_of(start, quarter), count * quarter)]
-
-        copies = {}
-
-        def add(name, src, dst, device):
-            i = len(copies)
-            copies[name] = Send(src, dst, w_send.at[which, i], w_recv.at[which, i], device)
-
-        add("up", part(here, 0, 2), part(there_up, 0, 2), (img, next_t))
-        add("down", part(here, 0, 2), part(there_down, 0, 2), (img, prev_t))
-        add("far_up", part(before, 0, 1), part(before if far_there is None else far_there, 0, 1), (img, next_t))
-        add("far_down", part(after, 1, 1), part(after if far_there is None else far_there, 1, 1), (img, prev_t))
-        add("before", part(before, 0, 2), part(before, 0, 2), sibling)
-        add("after", part(after, 0, 2), part(after, 0, 2), sibling)
-        add("far", part(far_here, 0, 2), part(far_here, 0, 2), sibling)
-        return copies
-
-    w_qkv = weight_copies(0, wqkv, 0, 3, 1, 1, 3, 2, 2)
-    w_out = weight_copies(1, wo, 0, 3, 1, 1, 3, 2, 2)
-    w_head = weight_copies(2, head, t, t, t, next_t, prev_t, far_t, None)
-
-    def first_sends(w):
-        w["up"].start()
-        w["down"].start()
-
-    def pass_on(w):
-        w["up"].wait_recv()
-        w["far_up"].start()
-        w["down"].wait_recv()
-        w["far_down"].start()
-        w["before"].start()
-        w["after"].start()
-
-    def pass_far(w):
-        w["far_up"].wait_recv()
-        w["far_down"].wait_recv()
-        w["far"].start()
-
-    def arrive(w, name):
-        w[name].wait_recv()
-
-    for i in (2, 3, 4):
-        loads[i].wait()
-    first_sends(w_qkv)
     loads[6].wait()
     first_sends(w_out)
 
@@ -341,12 +344,11 @@
     for h, start, width in going:
         if h == len(going) - 1:
             pass_on(w_qkv)
-            pass_on(w_out)
         z_copies[h].wait_recv()
         got = dot(turn_mat, zr[h][...].reshape(slots, width))
         ys[h][...] = got.astype(BF16).reshape(nd, tk, nz, width)
         y_copies.append(send_y(ys, yr, y_sem, h))
-    pass_far(w_qkv)
+    pass_on(w_out)
 
     x_copies = []
     for h, start, width in going:
@@ -356,6 +358,7 @@
             xs[h][:, ch] = got.astype(BF16).reshape(tp, 2 * pp, width)
         x_copies.append(send_x(xs, xr, x_sem, h))
 
+    pass_far(w_qkv)
     pass_far(w_out)
     loads[7].wait()
     first_sends(w_head)
@@ -373,23 +376,29 @@
     r0, r1 = iota((heads * rows, rows), 0) % rows, iota((heads * rows, rows), 1)
     seen = (r0 % pp == r1 % pp) & ((r0 // pp) % 2 != (r1 // pp) % 2)
     lane_head = iota((rows, gw), 1) // HEAD_DIM
-    mixed = jnp.zeros((rows, dm), F32)
-    for k, name in ((0, None), (3, "before"), (1, "after"), (2, "far")):
+    order = ((0, None), (3, "before"), (1, "after"), (2, "far"))
+    shares = []
+    for k, name in order:
         if name:
             arrive(w_qkv, name)
-        keys = dot_t(nk, wqkv[k, 0:gw]).astype(BF16)
-        values = dot_t(nk, wqkv[k, gw : 2 * gw]).astype(BF16)
-        query = (dot_t(nq, wqkv[k, 2 * gw : 3 * gw]) * HEAD_DIM ** (-0.5)).astype(BF16)
+        both = dot(nk, wqkv[k, :, 0 : 2 * gw]).astype(BF16)
+        keys, values = both[:, 0:gw], both[:, gw:]
+        query = (dot(nq, wqkv[k, :, 2 * gw :])[:, 0:gw] * HEAD_DIM ** (-0.5)).astype(BF16)
+        shares.append((keys, values, query))
+    for k, name in order[1:]:
+        arrive(w_out, name)
+    ones = jnp.ones((rows, gw), BF16)
+    mixed = jnp.zeros((rows, dm), F32)
+    for (k, _), (keys, values, query) in zip(order, shares):
         each = [jnp.where(lane_head == h, query, jnp.zeros_like(query)) for h in range(heads)]
         scores = jnp.where(seen, dot_t(jnp.concatenate(each, axis=0), keys), -1e38)
-        raised = jnp.exp(scores - jnp.max(scores, axis=-1, keepdims=True))
-        weights = raised * (1.0 / jnp.sum(raised, axis=-1, keepdims=True))
-        found = dot(weights.astype(BF16), values)
-        attended = found[0:rows]
+        raised = jnp.exp(scores - jnp.max(scores, axis=-1, keepdims=True)).astype(BF16)
+        found, total = dot(raised, values), dot(raised, ones)
+        attended, mass = found[0:rows], total[0:rows]
         for h in range(1, heads):
             attended = jnp.where(lane_head == h, found[h * rows : (h + 1) * rows], attended)
-        if name:
-            arrive(w_out, name)
+            mass = jnp.where(lane_head == h, total[h * rows : (h + 1) * rows], mass)
+        attended = attended / mass
         mixed = mixed + dot(attended.astype(BF16), wo[k]).astype(BF16).astype(F32)
     normed = norm_base(x + mixed) * gain_o[...].astype(F32).reshape(1, dm)
     for h, start, width in coming:
@@ -425,9 +434,13 @@
     for r in range(tp):
         oout[r] = maps[:, r * cols : (r + 1) * cols].reshape(tk, imgs, cols)
     others = [lax.rem(t + r, tp) for r in sorted(range(1, tp), key=lambda r: abs(2 * r - tp))]
-    Swap(oout, out_ref, o_sem, t, [(other, t, (img, other)) for other in others], o_own).wait_recv()
-
-    for wait in sent:
+    earlier = len(sent)
+    last = Swap(oout, out_ref, o_sem, t, [(other, t, (img, other)) for other in others], o_own)
+
+    for wait in sent[:earlier]:
+        wait()
+    last.wait_recv()
+    for wait in sent[earlier:]:
         wait()
 
 
@@ -464,6 +477,7 @@
     def buffers(widths, *shape):
         return tuple(pltpu.VMEM((*shape, width), BF16) for width in widths)
 
+    wide = -(-3 * gw // 128) * 128
     swap_z = nz, tk * nd
     swap_y = nd, tk, nz
     swap_x = tp, tk, 2 * pp
@@ -480,7 +494,8 @@
             pltpu.VMEM((imgs * toks, de), BF16),
             pltpu.VMEM(pairs.shape, jnp.int32),
             pltpu.VMEM(embed_w.shape, BF16),
-            pltpu.VMEM((tp, 3 * gw, dm), BF16),
+            pltpu.VMEM((wide, dm), BF16),
+            pltpu.VMEM((tp, dm, wide), BF16),
             pltpu.VMEM((tp, gw, dm), BF16),
             pltpu.VMEM((tp, gw, tp * cols), BF16),
             buffers(FORWARD, *swap_z),

time: 81.2 us -> 79.7 us (0.982)
  Pallas kernels: 79.5 us -> 77.7 us
    pallas_call x1, Pallas kernels: 79.5 us -> 77.7 us  [shards(): pl.pallas_call(functools.partial(body, dims), name='sublayer', out_shape=...]
where the time goes in v5:
time: 79.7 us; the launch traced here: 79.2 us
  Pallas kernels  77.7 us (97%)
  local copies, waits for them, and re-layouts  1.49 us (2%)
    pallas_call x1, Pallas kernels, shards(): pl.pallas_call(functools.partial(body, dims), name='sublayer', out_shape=...  77.7 us

profile of v5, /device:TPU:1, one launch (start us, length us, event | category | flops | bytes accessed | tf_op | source)
XLA Modules:
  0.0 79.2 jit_solution(6874820104854084312)
XLA Ops:
  0.0 77.7 %sublayer.1 = bf16[4,2,16,256]{3,2,1,0:T(8,128)(2,1)} custom-call(bf16[128,1024]{1,0:T(8,128)(2,1)} %bitcast.14, s32[32,2,128]{2,1,0:T(2,128)} %bitcast.16, bf16[1024,768]{1,0:T(8,128)(2,1)} %embed_hbm.1, bf16[768]{0:T(1024)(128)(2,1)} %gain_q_hbm.1, bf16[768]{0:T(1024)(128)(2,1)} %gain_k_hbm.1, bf16[768]{0:T(1024)(128)(2,1)} %gain_o_hbm.1, ...), custom_call_target="tpu_custom_call" | custom-call | tf_op jit(solution)/shard_map/sublayer/pallas_call | solution.py:484
  77.7 1.5 %copy.14 = bf16[8,16,256]{2,0,1:T(8,128)(2,1)} copy(bf16[8,16,256]{2,1,0:T(8,128)(2,1)} %bitcast.15) | data formatting | bytes 131072 | tf_op jit(solution)/shard_map/reshape | solution.py:543

commit v6 on v5

--- a/solution.py
+++ b/solution.py
@@ -306,10 +306,10 @@
             for k in (reach, nz - reach):
                 pl.semaphore_signal(far_sem, inc=1, device_id=at_z_of(k), device_id_type=MESH)
             first_sends(w_qkv)
-        z_copies.append(send_z(zs, zr, z_sem, h, near, far))
+        z_copies.append(send_z(zs, zr, z_sem, h, near if h == 0 else far_first, far if h == 0 else ()))
         if h == 0:
             pl.semaphore_wait(far_sem, 2)
-        z_copies[h].start(z_places(far))
+            z_copies[h].start(z_places(far))
 
     loads[6].wait()
     first_sends(w_out)

time: 79.7 us -> 79.1 us (level)
  no operation moved by 1% of the time
where the time goes in v6:
time: 79.1 us; the launch traced here: 78.9 us
  Pallas kernels  77.4 us (98%)
  local copies, waits for them, and re-layouts  1.49 us (2%)
    pallas_call x1, Pallas kernels, shards(): pl.pallas_call(functools.partial(body, dims), name='sublayer', out_shape=...  77.4 us

profile of v6, /device:TPU:1, one launch (start us, length us, event | category | flops | bytes accessed | tf_op | source)
XLA Modules:
  0.0 78.9 jit_solution(8724132511341261078)
XLA Ops:
  0.0 77.4 %sublayer.1 = bf16[4,2,16,256]{3,2,1,0:T(8,128)(2,1)} custom-call(bf16[128,1024]{1,0:T(8,128)(2,1)} %bitcast.14, s32[32,2,128]{2,1,0:T(2,128)} %bitcast.16, bf16[1024,768]{1,0:T(8,128)(2,1)} %embed_hbm.1, bf16[768]{0:T(1024)(128)(2,1)} %gain_q_hbm.1, bf16[768]{0:T(1024)(128)(2,1)} %gain_k_hbm.1, bf16[768]{0:T(1024)(128)(2,1)} %gain_o_hbm.1, ...), custom_call_target="tpu_custom_call" | custom-call | tf_op jit(solution)/shard_map/sublayer/pallas_call | solution.py:484
  77.5 1.5 %copy.14 = bf16[8,16,256]{2,0,1:T(8,128)(2,1)} copy(bf16[8,16,256]{2,1,0:T(8,128)(2,1)} %bitcast.15) | data formatting | bytes 131072 | tf_op jit(solution)/shard_map/reshape | solution.py:543
